TPU v7x, 128 devices: a whole 4x4x4 slice. The times are simulated.
128 devices in a mesh: section: 2 (over core), node: 16 (over y, x), local: 4 (over z).
Axes of the slice: x: 4, y: 4, z: 4, core: 2. Of those that a mesh axis runs over, the one named last changes fastest.
Arguments:
- grad_out: bfloat16 [4096, 7168], P(('section', 'node'), 'local'), may hold values from -6 to 6
- node_ids: int32 [4096, 4], P(('section', 'node')), may hold values from 0 to 15, as said below
- expert_ids: int32 [4096, 6], P(('section', 'node')), may hold values from 0 to 31, as said below
- gate_probs: float32 [4096, 6], P(('section', 'node')), may hold values from 0.05 to 0.5
- gate_pre: bfloat16 [64, 1024, 1024], P(('section', 'node'), None, 'local'), may hold values from -6 to 6
- up_pre: bfloat16 [64, 1024, 1024], P(('section', 'node'), None, 'local'), may hold values from -6 to 6
- gate_weight: bfloat16 [64, 7168, 1024], P(('section', 'node'), 'local'), may hold values from -0.0625 to 0.0625
- up_weight: bfloat16 [64, 7168, 1024], P(('section', 'node'), 'local'), may hold values from -0.0625 to 0.0625
- down_weight: bfloat16 [64, 1024, 7168], P(('section', 'node'), None, 'local'), may hold values from -0.1875 to 0.1875
Outputs:
- handed: bfloat16 [4096, 7168], P(('section', 'node'), 'local')
- prob_grad: float32 [4096, 6], P(('section', 'node'))
Inputs may be any that keep to these rules, and one draw needn't show every extreme that they name: `node_ids`: each row names 4 different node groups of its section. Of the 128 tokens of one block, at most 64 name any one node group, and in each section one node group is named by exactly 64 tokens of every block. `expert_ids`: each row names 6 different experts of its section; expert e belongs to node group e // 2, each named expert belongs to one of the row's node groups, and each of the row's node groups holds at least one named expert.
All inputs are finite; a program needn't handle non-finite values.
Results may differ from a plain program's by a relative error of at most 0.02.
Values may be sent and summed in bfloat16 or wider, within the bound.
A program may use at most 128 MiB of HBM per device.

v0:
```python
import jax
import jax.numpy as jnp
from jax import lax
from jax.sharding import PartitionSpec as P


def passed_along(value, axis, steps):
    count = lax.axis_size(axis)
    pairs = [(source, (source + steps) % count) for source in range(count)]
    return lax.ppermute(value, axis, pairs)


def silu_backward(raw_grad, weight_rows, gate_pre, up_pre):
    gate_value = gate_pre.astype(jnp.float32)
    up_value = up_pre.astype(jnp.float32)
    sigmoid_gate = jax.nn.sigmoid(gate_value)
    active = gate_value * sigmoid_gate
    prob_part = jnp.sum(raw_grad * active * up_value, axis=2)
    scaled = raw_grad * weight_rows[:, :, None]
    gate_grad = (
        scaled * up_value * sigmoid_gate * (1.0 + gate_value * (1.0 - sigmoid_gate))
    ).astype(jnp.bfloat16)
    up_grad = (scaled * active).astype(jnp.bfloat16)
    return (prob_part, gate_grad, up_grad)


def shards(
    grad_out,
    node_ids,
    expert_ids,
    gate_probs,
    gate_pre,
    up_pre,
    gate_weight,
    up_weight,
    down_weight,
):
    node_count = lax.axis_size("node")
    token_count = grad_out.shape[0]
    slice_width = grad_out.shape[1]
    experts_here = gate_weight.shape[0]
    rows_node = gate_pre.shape[1]
    capacity = rows_node // node_count
    node_range = jnp.arange(node_count, dtype=jnp.int32)
    member = jnp.any(node_ids[:, :, None] == node_range[None, None, :], axis=1).astype(jnp.int32)
    position = jnp.cumsum(member, axis=0, dtype=jnp.int32) - member
    slot_range = jnp.arange(capacity, dtype=jnp.int32)
    chosen = (position[:, :, None] == slot_range[None, None, :]) & (member[:, :, None] > 0)
    select_half = chosen.astype(jnp.bfloat16).reshape(token_count, node_count * capacity)
    select_full = chosen.astype(jnp.float32)
    expert_range = (
        node_range[:, None] * experts_here + jnp.arange(experts_here, dtype=jnp.int32)[None, :]
    )
    matched = expert_ids[:, :, None, None] == expert_range[None, None, :, :]
    token_mass = jnp.sum(jnp.where(matched, gate_probs[:, :, None, None], 0.0), axis=1)
    outgoing = lax.dot_general(
        select_half, grad_out, (((0,), (0,)), ((), ())), preferred_element_type=jnp.float32
    ).astype(jnp.bfloat16)
    outgoing_mass = jnp.einsum(
        "tmc,tme->mce", select_full, token_mass, precision=lax.Precision.HIGHEST
    ).astype(jnp.bfloat16)
    arrived, arrived_mass = (
        lax.all_to_all(
            outgoing.reshape(node_count, capacity, slice_width),
            "node",
            split_axis=0,
            concat_axis=0,
            tiled=True,
        ),
        lax.all_to_all(outgoing_mass, "node", split_axis=0, concat_axis=0, tiled=True),
    )
    arrived = arrived.reshape(rows_node, slice_width)
    weight_rows = arrived_mass.reshape(rows_node, experts_here).astype(jnp.float32).T
    saved_gate, saved_up = (
        lax.all_gather(gate_pre, "local", axis=2, tiled=True),
        lax.all_gather(up_pre, "local", axis=2, tiled=True),
    )
    partial_value = jnp.einsum(
        "rd,efd->erf", arrived, down_weight, preferred_element_type=jnp.float32
    )
    raw_grad = lax.psum(partial_value.astype(jnp.bfloat16), "local").astype(jnp.float32)
    prob_rows, gate_grad, up_grad = silu_backward(raw_grad, weight_rows, saved_gate, saved_up)
    returned = jnp.einsum("erf,edf->rd", gate_grad, gate_weight, preferred_element_type=jnp.float32)
    returned = returned + jnp.einsum(
        "erf,edf->rd", up_grad, up_weight, preferred_element_type=jnp.float32
    )
    returned_half = returned.astype(jnp.bfloat16)
    prob_half = prob_rows.T.astype(jnp.bfloat16)
    back_rows, back_prob = (
        lax.all_to_all(
            returned_half.reshape(node_count, capacity, slice_width),
            "node",
            split_axis=0,
            concat_axis=0,
            tiled=True,
        ),
        lax.all_to_all(
            prob_half.reshape(node_count, capacity, experts_here),
            "node",
            split_axis=0,
            concat_axis=0,
            tiled=True,
        ),
    )
    input_grad = jnp.dot(
        select_half,
        back_rows.reshape(node_count * capacity, slice_width),
        preferred_element_type=jnp.float32,
    ).astype(jnp.bfloat16)
    token_prob = jnp.einsum(
        "tmc,mce->tme", select_full, back_prob.astype(jnp.float32), precision=lax.Precision.HIGHEST
    )
    prob_grad = jnp.sum(jnp.where(matched, token_prob[:, None, :, :], 0.0), axis=(2, 3))
    handed = passed_along(input_grad, "section", -1)
    return (handed, prob_grad)


def solution(mesh):
    return jax.shard_map(
        shards,
        mesh=mesh,
        in_specs=(
            P(("section", "node"), "local"),
            P(("section", "node"), None),
            P(("section", "node"), None),
            P(("section", "node"), None),
            P(("section", "node"), None, "local"),
            P(("section", "node"), None, "local"),
            P(("section", "node"), "local", None),
            P(("section", "node"), "local", None),
            P(("section", "node"), None, "local"),
        ),
        out_specs=(P(("section", "node"), "local"), P(("section", "node"), None)),
        check_vma=False,
    )
```

profile of v0, /device:TPU:1, one launch (start us, length us, event | category | flops | bytes accessed | tf_op | source)
XLA Modules:
  0.0 340.6 jit_solution(10588264419634482360)
XLA Ops:
  7.2 0.0 copy-start
  7.2 0.0 all-gather.5.cloned.1.call-start
  7.2 0.7 all-gather.5.cloned.1.call-update
  7.9 0.0 all-gather.3.cloned.1.call-start
  8.0 0.7 all-gather.3.cloned.1.call-update
  8.7 0.0 all-reduce.2.cloned.1.call-start
  8.7 0.1 eq.58
  8.8 0.7 fusion.29
  9.5 0.1 copy.39
  9.6 0.1 copy.41
  9.7 0.2 reduce_window_sum.11
  9.9 0.1 copy.40
  9.9 0.0 copy-start.4
  9.9 0.2 fusion.20
  10.2 0.0 copy-done
  10.2 1.1 convolution_convert_fusion
  11.3 51.7 %all_to_all.20 = bf16[16,64,1792]{2,1,0:T(8,128)(2,1)S(1)} all-to-all(bf16[16,64,1792]{2,1,0:T(8,128)(2,1)S(1)} %bitcast.41), channel_id=1, replica_groups=mesh['section'=2,'node'=16,'local'=4] {'node'}, dimensions={0} | all-to-all | bytes 7340032 | tf_op jit(solution)/shard_map/all_to_all | solution.py:63
  63.0 0.0 copy-done.4
  63.0 9.4 %convert_bitcast_fusion = bf16[2,1024,1024]{2,1,0:T(8,128)(2,1)} fusion(bf16[1024,1792,1]{1,0,2:T(8,128)(2,1)S(1)} %bitcast.43, bf16[2,1024,1792]{2,1,0:T(8,128)(2,1)S(1)} %copy-done.4), kind=kOutput, calls=%fused_computation.20 | convolution fusion | flops 7518289920 | bytes 15204352 | tf_op jit(solution)/shard_map/rd,efd->erf/dot_general | solution.py:78
  72.4 0.0 all-reduce.2.cloned.1.call-update
  72.4 0.0 copy-start.2
  72.5 0.0 copy-start.3
  72.5 0.0 all-gather.5.cloned.1.call-done
  72.5 46.4 %all-gather.3.cloned.1.call-done = bf16[2,1024,1024]{2,1,0:T(8,128)(2,1)} async-done(((bf16[2,1024,256]{2,1,0:T(8,128)(2,1)}), bf16[2,1024,1024]{2,1,0:T(8,128)(2,1)}) %all-gather.3.cloned.1.call-update) | async-done | bytes 4194320 | tf_op jit(solution)/shard_map/all_gather | solution.py:76
  118.9 97.1 %all-reduce.2.cloned.1.call-done = bf16[2,1024,1024]{2,1,0:T(8,128)(2,1)} async-done(((bf16[2,1024,1024]{2,1,0:T(8,128)(2,1)}), bf16[2,1024,1024]{2,1,0:T(8,128)(2,1)}) %all-reduce.2.cloned.1.call-update) | async-done | bytes 4194320 | tf_op jit(solution)/shard_map/psum | solution.py:81
  216.0 6.2 %fusion.5 = bf16[2,1024]{1,0:T(2,128)(2,1)S(1)} fusion(bf16[2,1024,1024]{2,1,0:T(8,128)(2,1)} %all-gather.3.cloned.1.call-done, bf16[2,1024,1024]{2,1,0:T(8,128)(2,1)} %all-reduce.2.cloned.1.call-done, bf16[2,1024,1024]{2,1,0:T(8,128)(2,1)} %all-gather.5.cloned.1.call-done), kind=kLoop, calls=%fused_computation.12 | loop fusion | flops 20969472 | bytes 12587008 | tf_op jit(solution)/shard_map/reduce_sum | solution.py:18
  222.3 0.1 reshape.72
  222.4 0.6 copy.44
  223.0 6.5 %all-to-all-start.3 = ((bf16[16,64,2]{1,2,0:T(2,128)(2,1)}), bf16[16,64,2]{1,2,0:T(2,128)(2,1)S(1)}, u32[]{:S(2)}, u32[]{:S(2)}) async-start(bf16[16,64,2]{1,2,0:T(2,128)(2,1)} %copy.44), calls=%async_computation.3 | async-start | bytes 16384 | tf_op jit(solution)/shard_map/all_to_all | solution.py:97
  229.5 6.3 %all-to-all-done.3 = bf16[16,64,2]{1,2,0:T(2,128)(2,1)S(1)} async-done(((bf16[16,64,2]{1,2,0:T(2,128)(2,1)}), bf16[16,64,2]{1,2,0:T(2,128)(2,1)S(1)}, u32[]{:S(2)}, u32[]{:S(2)}) %all-to-all-start.3) | async-done | bytes 4128 | tf_op jit(solution)/shard_map/all_to_all | solution.py:97
  235.8 0.2 convolution_bitcast_fusion.1
  236.1 0.0 copy-done.2
  236.1 0.0 copy-done.3
  236.1 0.7 fusion.28
  236.8 0.5 convolution_convert_fusion.1
  237.3 9.1 %all_to_all.21 = bf16[16,64,2]{1,2,0:T(2,128)(2,1)S(1)} all-to-all(bf16[16,64,2]{1,2,0:T(2,128)(2,1)S(1)} %convolution_convert_fusion.1), channel_id=1, replica_groups=mesh['section'=2,'node'=16,'local'=4] {'node'}, dimensions={0} | all-to-all | bytes 8192 | tf_op jit(solution)/shard_map/all_to_all | solution.py:70
  246.4 0.1 reshape.73
  246.5 0.0 copy-start.1
  246.5 18.5 %fusion.13 = f32[1024,1792,1]{1,0,2:T(8,128)} fusion(bf16[2,1792,1024]{2,1,0:T(8,128)(2,1)} %param.15, bf16[2,1024,1024]{2,1,0:T(8,128)(2,1)} %all-gather.3.cloned.1.call-done, bf16[2,1024,1024]{2,1,0:T(8,128)(2,1)} %all-reduce.2.cloned.1.call-done, bf16[2,1024,1024]{2,1,0:T(8,128)(2,1)} %all-gather.5.cloned.1.call-done, f32[2,1024]{1,0:T(2,128)S(1)} %bitcast.45), kind=kOutput, calls=%fused_computation.21 | convolution fusion | flops 7545552896 | bytes 27271168 | tf_op jit(solution)/shard_map/erf,edf->rd/dot_general | solution.py:83
  264.9 0.0 copy-done.1
  264.9 16.2 %fusion.10 = bf16[1024,1792]{1,0:T(8,128)(2,1)} fusion(f32[1024,1792,1]{1,0,2:T(8,128)} %fusion.13, bf16[2,1792,1024]{2,1,0:T(8,128)(2,1)} %param.16, bf16[2,1024,1024]{2,1,0:T(8,128)(2,1)} %all-reduce.2.cloned.1.call-done, f32[2,1024]{1,0:T(2,128)S(1)} %bitcast.46, bf16[2,1024,1024]{2,1,0:T(8,128)(2,1)S(1)} %copy-done.1), kind=kOutput, calls=%fused_computation.18 | convolution fusion | flops 7538737152 | bytes 26746880 | tf_op jit(solution)/shard_map/erf,edf->rd/dot_general | solution.py:84
  281.1 45.3 %all_to_all.22 = bf16[16,64,1792]{2,1,0:T(8,128)(2,1)S(1)} all-to-all(bf16[16,64,1792]{2,1,0:T(8,128)(2,1)} %bitcast.42), channel_id=1, replica_groups=mesh['section'=2,'node'=16,'local'=4] {'node'}, dimensions={0} | all-to-all | bytes 7340032 | tf_op jit(solution)/shard_map/all_to_all | solution.py:90
  326.4 0.7 fusion.15
  327.1 4.7 %collective-permute-start = (bf16[128,1792]{1,0:T(8,128)(2,1)S(1)}, bf16[128,1792]{1,0:T(8,128)(2,1)S(1)}, u32[]{:S(2)}, u32[]{:S(2)}) collective-permute-start(bf16[128,1792]{1,0:T(8,128)(2,1)S(1)} %fusion.15), channel_id=1, source_target_pairs={{0,64},{64,0},{1,65},{65,1},{2,66},{66,2},{3,67},{67,3},{4,68},{68... | collective-permute-start | bytes 1376264 | tf_op jit(solution)/shard_map/ppermute | solution.py:10
  331.8 1.4 collective-permute-done
  333.3 0.8 copy.53
  (7 shorter events, 0.0 us)
Async XLA Ops:
  7.2 3.0 copy-start
  7.2 65.3 %all-gather.5.cloned.1.call-start = ((), (), s32[]{:S(2)}) async-start(), calls=%async_computation.6 | async-start | bytes 5242880 | tf_op jit(solution)/shard_map/all_gather | solution.py:75
  7.9 111.0 %all-gather.3.cloned.1.call-start = ((), (), s32[]{:S(2)}) async-start(), calls=%async_computation.5 | async-start | bytes 5242880 | tf_op jit(solution)/shard_map/all_gather | solution.py:76
  8.7 207.4 %all-reduce.2.cloned.1.call-start = ((), (), s32[]{:S(2)}) async-start(), calls=%async_computation.4 | async-start | bytes 8388608 | tf_op jit(solution)/shard_map/psum | solution.py:81
  9.9 53.1 %copy-start.4 = (bf16[2,1024,1792]{2,1,0:T(8,128)(2,1)S(1)}, bf16[2,1024,1792]{2,1,0:T(8,128)(2,1)}, u32[]{:S(2)}) copy-start(bf16[2,1024,1792]{2,1,0:T(8,128)(2,1)} %param.17) | copy-start | bytes 22020100
  72.4 163.6 %copy-start.2 = (s32[128,6]{0,1:T(8,128)S(1)}, s32[128,6]{0,1:T(8,128)}, u32[]{:S(2)}) copy-start(s32[128,6]{0,1:T(8,128)} %param.11) | copy-start | bytes 9220
  72.5 163.6 %copy-start.3 = (f32[128,6]{0,1:T(8,128)S(1)}, f32[128,6]{0,1:T(8,128)}, u32[]{:S(2)}) copy-start(f32[128,6]{0,1:T(8,128)} %param.12) | copy-start | bytes 9220
  223.0 12.9 %all-to-all-start.3 = ((bf16[16,64,2]{1,2,0:T(2,128)(2,1)}), bf16[16,64,2]{1,2,0:T(2,128)(2,1)S(1)}, u32[]{:S(2)}, u32[]{:S(2)}) async-start(bf16[16,64,2]{1,2,0:T(2,128)(2,1)} %copy.44), calls=%async_computation.3 | async-start | bytes 16384 | tf_op jit(solution)/shard_map/all_to_all | solution.py:97
  246.5 18.5 %copy-start.1 = (bf16[2,1024,1024]{2,1,0:T(8,128)(2,1)S(1)}, bf16[2,1024,1024]{2,1,0:T(8,128)(2,1)}, u32[]{:S(2)}) copy-start(bf16[2,1024,1024]{2,1,0:T(8,128)(2,1)} %all-gather.5.cloned.1.call-done) | copy-start | bytes 12582916
  327.1 6.2 %collective-permute-start = (bf16[128,1792]{1,0:T(8,128)(2,1)S(1)}, bf16[128,1792]{1,0:T(8,128)(2,1)S(1)}, u32[]{:S(2)}, u32[]{:S(2)}) collective-permute-start(bf16[128,1792]{1,0:T(8,128)(2,1)S(1)} %fusion.15), channel_id=1, source_target_pairs={{0,64},{64,0},{1,65},{65,1},{2,66},{66,2},{3,67},{67,3},{4,68},{68... | collective-permute-start | bytes 1376264 | tf_op jit(solution)/shard_map/ppermute | solution.py:10
Sparse Core Ops, SparseCore 0:
  9.7 54.5 all-gather.4
  65.9 52.9 all-gather.2
  121.3 94.7 all-reduce.1
where the time goes:
time: 341 us
  waiting for transfers between devices  153 us (45%)
  blocking collectives  106 us (31%)
  matrix products  46.5 us (14%)
  between operations  13.9 us (4%)
  starting transfers between devices  11.4 us (3%)
  other arithmetic  8.06 us (2%)
    psum x1, waiting for transfers between devices, shards(): lax.psum(partial_value.astype(jnp.bfloat16), 'local').astype(jnp.float32)  97.1 us
    all_to_all x1, blocking collectives, shards(): lax.all_to_all(outgoing.reshape(node_count, capacity, slice_width), 'node...  51.7 us
    all_gather x1, waiting for transfers between devices, shards(): lax.all_gather(up_pre, 'local', axis=2, tiled=True)  46.4 us
    all_to_all x1, blocking collectives, shards(): lax.all_to_all(returned_half.reshape(node_count, capacity, slice_width),...  45.3 us
    dot_general x1, matrix products, shards(): jnp.einsum('erf,edf->rd', gate_grad, gate_weight, preferred_element_type=...  18.5 us
    dot_general x1, matrix products, shards(): jnp.einsum('erf,edf->rd', up_grad, up_weight, preferred_element_type=jnp....  16.2 us
    dot_general x1, matrix products, shards(): jnp.einsum('rd,efd->erf', arrived, down_weight, preferred_element_type=jn...  9.39 us
    all_to_all x1, blocking collectives, shards(): lax.all_to_all(outgoing_mass, 'node', split_axis=0, concat_axis=0, tiled=...  9.12 us
  transfers between devices with their start and end apart: 5, of which 4 were waited for; matrix products, arithmetic and copies ran while one was open for 4% of the time, Pallas kernels for 0%

commit v1 on v0

v1 whole, which is shorter than its diff:
```python
import functools

import jax
import jax.numpy as jnp
from jax import lax
from jax.experimental import pallas as pl
from jax.experimental.pallas import tpu as pltpu
from jax.sharding import PartitionSpec as P

MESH = pl.DeviceIdType.MESH
SIDE = 4
NODES = 16
CAP = 64
UNIT = 16
TILE = 128
EXTRA = 128
CHUNKS = (8, 8, 16, 16, 8, 8)


def offset(o):
    half = o // 8
    rest = o % 8
    dy = rest // 2
    dx = (2 * (rest % 2) + dy % 2 + half) % SIDE
    return dy, dx


def nt_dot(a, b):
    return lax.dot_general(a, b, (((1,), (1,)), ((), ())), preferred_element_type=jnp.float32)


def kernel(
    x_ref,
    nodes_ref,
    experts_ref,
    probs_ref,
    gate_pre_ref,
    up_pre_ref,
    gate_w_ref,
    up_w_ref,
    down_w_ref,
    handed_ref,
    prob_ref,
    gate_pre,
    up_pre,
    gate_w,
    up_w,
    down_w,
    x_ext,
    sel,
    sel_other,
    out_rows,
    in_rows,
    part,
    rs_far,
    rs_near,
    grads,
    ret_rows,
    back_rows,
    acc,
    mine,
    total,
    load_sem,
    disp_send,
    disp_recv,
    sel_send,
    sel_recv,
    rs_send,
    rs_far_recv,
    rs_near_recv,
    ag_send,
    ag_recv,
    ag_far_recv,
    ret_send,
    ret_recv,
    tok_send,
    tok_recv,
):
    s = lax.axis_index("section")
    n = lax.axis_index("node")
    z = lax.axis_index("local")
    other = 1 - s
    my, mx = n // SIDE, n % SIDE
    up = lax.rem(z + 1, SIDE)
    down = lax.rem(z + 3, SIDE)
    tokens, width = x_ref.shape
    full = width + EXTRA
    rows_node = gate_pre.shape[1]
    hidden = gate_pre.shape[2]

    def node_plus(o):
        dy, dx = offset(o)
        return ((my + dy) % SIDE) * SIDE + (mx + dx) % SIDE

    def node_minus(o):
        dy, dx = offset(o)
        return ((my + SIDE - dy) % SIDE) * SIDE + (mx + SIDE - dx) % SIDE

    def rows_of(start, count):
        return pl.ds(pl.multiple_of(start, UNIT), count)

    def quarter(index):
        return pl.ds(pl.multiple_of(index * hidden, hidden), hidden)

    loads = [
        pltpu.make_async_copy(src, dst, load_sem.at[i])
        for i, (src, dst) in enumerate(
            (
                (down_w_ref, down_w),
                (gate_pre_ref, gate_pre),
                (up_pre_ref, up_pre),
                (gate_w_ref, gate_w),
                (up_w_ref, up_w),
            )
        )
    ]
    loads[0].start()

    barrier = pltpu.get_barrier_semaphore()

    def greet(section, node, local):
        pl.semaphore_signal(
            barrier,
            inc=1,
            device_id={"section": section, "node": node, "local": local},
            device_id_type=MESH,
        )

    greet(s, n, up)
    greet(s, n, down)
    for k in range(1, SIDE):
        greet(other, n, (z + k) % SIDE)

    @pl.loop(1, NODES)
    def _(o):
        greet(s, node_plus(o), z)

    @pl.loop(0, NODES)
    def _(o):
        greet(other, node_plus(o), z)

    for load in loads[1:]:
        load.start()

    lane = lax.broadcasted_iota(jnp.int32, (tokens, EXTRA), 1)
    mass = jnp.zeros((tokens, EXTRA), jnp.float32)
    for k in range(experts_ref.shape[1]):
        mass = mass + jnp.where(lane == experts_ref[:, k : k + 1], probs_ref[:, k : k + 1], 0.0)
    x_ext[:, width:] = mass.astype(jnp.bfloat16)
    x_ext[:, :width] = x_ref[...]

    before = (
        lax.broadcasted_iota(jnp.int32, (tokens, tokens), 1)
        < lax.broadcasted_iota(jnp.int32, (tokens, tokens), 0)
    )
    before = jnp.where(before, 1.0, 0.0).astype(jnp.bfloat16)

    pl.semaphore_wait(barrier, 2 + (SIDE - 1) + (NODES - 1) + NODES)

    @pl.loop(0, rows_node // TILE)
    def _(t):
        column = lax.broadcasted_iota(jnp.int32, (tokens, TILE), 1) + t * TILE
        u = column >> 4
        o = u & 15
        rest = o & 7
        dy = rest >> 1
        dx = (2 * (rest & 1) + (dy & 1) + (o >> 3)) & 3
        node = ((my + dy) & 3) * SIDE + ((mx + dx) & 3)
        slot = (u >> 4) * UNIT + (column & 15)
        member = nodes_ref[:, 0:1] == node
        for k in range(1, nodes_ref.shape[1]):
            member = member | (nodes_ref[:, k : k + 1] == node)
        member = jnp.where(member, 1.0, 0.0)
        position = jnp.dot(
            before, member.astype(jnp.bfloat16), preferred_element_type=jnp.float32
        )
        chosen = jnp.where(position == slot.astype(jnp.float32), member, 0.0)
        sel[t] = chosen.astype(jnp.bfloat16)
        picked = jnp.dot(
            chosen.T.astype(jnp.bfloat16), x_ext[...], preferred_element_type=jnp.float32
        ).astype(jnp.bfloat16)
        first = rows_of(t * TILE, TILE)
        out_rows[first, :] = picked

        @pl.when(t % 2 == 0)
        def _():
            in_rows[rows_of(t * TILE, UNIT), :] = picked[:UNIT]

        @pl.loop(1 - t % 2, TILE // UNIT)
        def _(i):
            rows = rows_of(t * TILE + i * UNIT, UNIT)
            pltpu.make_async_remote_copy(
                src_ref=out_rows.at[rows],
                dst_ref=in_rows.at[rows],
                send_sem=disp_send,
                recv_sem=disp_recv.at[t],
                device_id={"section": s, "node": node_plus((t % 2) * 8 + i), "local": z},
                device_id_type=MESH,
            ).start()

    sel_copy = pltpu.make_async_remote_copy(
        src_ref=sel,
        dst_ref=sel_other,
        send_sem=sel_send,
        recv_sem=sel_recv,
        device_id={"section": other, "node": n, "local": z},
        device_id_type=MESH,
    )
    sel_copy.start()

    starts = [UNIT * sum(CHUNKS[:c]) for c in range(len(CHUNKS))]
    sizes = [UNIT * count for count in CHUNKS]

    def along_z(src, dst, send_sem, recv_sem, local):
        pltpu.make_async_remote_copy(
            src_ref=src,
            dst_ref=dst,
            send_sem=send_sem,
            recv_sem=recv_sem,
            device_id={"section": s, "node": n, "local": local},
            device_id_type=MESH,
        ).start()

    def landed(ref, sem):
        pltpu.make_async_copy(ref, ref, sem).wait()

    def multiply_down(c):
        begin, count = starts[c], sizes[c]
        rows = pl.ds(begin, count)
        for t in range(begin // TILE, (begin + count) // TILE):
            if t % 2 == 0:
                landed(in_rows.at[pl.ds(t * TILE + UNIT, TILE - UNIT)], disp_recv.at[t])
            else:
                landed(in_rows.at[pl.ds(t * TILE, TILE)], disp_recv.at[t])
        if c == 0:
            loads[0].wait()

        def products(first, last, step_of):
            @pl.loop(2 * first, 2 * last)
            def _(i):
                k, e = i // 2, i % 2
                step = step_of(k)
                weights = down_w[e, quarter((z + step) % SIDE), :]
                part[k, e, rows, :] = nt_dot(in_rows[rows, :width], weights).astype(jnp.bfloat16)

        products(0, 1, lambda k: 2)
        along_z(part.at[0, 0, rows], rs_far.at[0, rows], rs_send, rs_far_recv.at[c, 0], up)
        along_z(part.at[0, 1, rows], rs_far.at[1, rows], rs_send, rs_far_recv.at[c, 1], down)
        products(1, 3, lambda k: 2 * k - 1)
        along_z(part.at[1, 1, rows], rs_near.at[0, 1, rows], rs_send, rs_near_recv.at[c, 0, 1], up)
        along_z(
            part.at[2, 0, rows], rs_near.at[1, 0, rows], rs_send, rs_near_recv.at[c, 1, 0], down
        )
        products(3, 4, lambda k: 0)

    def add_far(c):
        rows = pl.ds(starts[c], sizes[c])
        for way, local in ((0, up), (1, down)):
            landed(rs_far.at[way, rows], rs_far_recv.at[c, way])
            part[1 + way, way, rows, :] = (
                part[1 + way, way, rows, :].astype(jnp.float32)
                + rs_far[way, rows, :].astype(jnp.float32)
            ).astype(jnp.bfloat16)
            along_z(
                part.at[1 + way, way, rows],
                rs_near.at[way, way, rows],
                rs_send,
                rs_near_recv.at[c, way, way],
                local,
            )

    def hidden_grads(c):
        begin, count = starts[c], sizes[c]
        rows = pl.ds(begin, count)
        for way in range(2):
            for e in range(2):
                landed(rs_near.at[way, e, rows], rs_near_recv.at[c, way, e])
        if c == 0:
            loads[1].wait()
            loads[2].wait()
        mine_columns = quarter(z)

        @pl.loop(begin // UNIT, (begin + count) // UNIT)
        def _(u):
            here = rows_of(u * UNIT, UNIT)
            saved = rows_of(node_minus(u % 16) * CAP + u // 16 * UNIT, UNIT)
            masses = in_rows[here, width:].astype(jnp.float32)
            expert = lax.broadcasted_iota(jnp.int32, (UNIT, EXTRA), 1)
            extra = jnp.zeros((UNIT, EXTRA), jnp.float32)
            for e in range(2):
                raw = (
                    part[3, e, here, :].astype(jnp.float32)
                    + rs_near[0, e, here, :].astype(jnp.float32)
                    + rs_near[1, e, here, :].astype(jnp.float32)
                )
                gate = gate_pre[e, saved, :].astype(jnp.float32)
                value = up_pre[e, saved, :].astype(jnp.float32)
                weight = jnp.sum(
                    jnp.where(expert == 2 * n + e, masses, 0.0), axis=1, keepdims=True
                )
                q = jax.nn.sigmoid(gate)
                active = gate * q
                prob = jnp.sum(raw * active * value, axis=1, keepdims=True)
                high = prob.astype(jnp.bfloat16).astype(jnp.float32)
                extra = jnp.where(expert == 2 * n + e, high, extra)
                extra = jnp.where(expert == 32 + 2 * n + e, prob - high, extra)
                scaled = raw * weight
                grads[2 * e, here, mine_columns] = (
                    scaled * value * q * (1.0 + gate * (1.0 - q))
                ).astype(jnp.bfloat16)
                grads[2 * e + 1, here, mine_columns] = (scaled * active).astype(jnp.bfloat16)
            ret_rows[here, width:] = extra.astype(jnp.bfloat16)

        for turn in range(2):
            for way, local in ((0, up), (1, down)):
                e = way ^ turn
                piece = grads.at[pl.ds(2 * e, 2), rows, mine_columns]
                along_z(piece, piece, ag_send, ag_recv.at[c, way, e], local)

    def send_on(c):
        rows = pl.ds(starts[c], sizes[c])
        for way, local, owner in ((0, up, down), (1, down, up)):
            piece = grads.at[pl.ds(2 * way, 2), rows, quarter(owner)]
            landed(piece, ag_recv.at[c, way, way])
            along_z(piece, piece, ag_send, ag_far_recv.at[c, way], local)

    def multiply_up(c):
        begin, count = starts[c], sizes[c]
        rows = pl.ds(begin, count)
        far = lax.rem(z + 2, SIDE)
        for way, owner in ((0, down), (1, up)):
            e = 1 - way
            landed(grads.at[pl.ds(2 * e, 2), rows, quarter(owner)], ag_recv.at[c, way, e])
            landed(grads.at[pl.ds(2 * way, 2), rows, quarter(far)], ag_far_recv.at[c, way])
        if c == 0:
            loads[3].wait()
            loads[4].wait()

        @pl.loop(0, width // 256)
        def _(i):
            features = pl.ds(pl.multiple_of(i * 256, 256), 256)
            ret_rows[rows, features] = (
                nt_dot(grads[0, rows, :], gate_w[0, features, :])
                + nt_dot(grads[1, rows, :], up_w[0, features, :])
                + nt_dot(grads[2, rows, :], gate_w[1, features, :])
                + nt_dot(grads[3, rows, :], up_w[1, features, :])
            ).astype(jnp.bfloat16)

        @pl.loop(begin // UNIT, (begin + count) // UNIT)
        def _(u):
            here = rows_of(u * UNIT, UNIT)
            pltpu.make_async_remote_copy(
                src_ref=ret_rows.at[here],
                dst_ref=back_rows.at[here],
                send_sem=ret_send,
                recv_sem=ret_recv.at[u // 8],
                device_id={"section": other, "node": node_minus(u % 16), "local": z},
                device_id_type=MESH,
            ).start()

    def combine(c):
        begin, count = starts[c], sizes[c]
        if c == 0:
            sel_copy.wait_recv()
        for t in range(begin // TILE, (begin + count) // TILE):
            rows = pl.ds(t * TILE, TILE)
            landed(back_rows.at[rows], ret_recv.at[t])

            @pl.loop(0, full // 384)
            def _(i):
                features = pl.ds(pl.multiple_of(i * 384, 128), 384)
                term = jnp.dot(
                    sel_other[t], back_rows[rows, features], preferred_element_type=jnp.float32
                )
                if t == 0:
                    acc[:, features] = term
                else:
                    acc[:, features] += term

    last = len(CHUNKS) - 1
    multiply_down(0)
    add_far(0)
    hidden_grads(0)
    for c in range(last + 1):
        if c > 0:
            if c < last:
                multiply_down(c + 1)
            hidden_grads(c)
        else:
            multiply_down(1)
        if c < last:
            add_far(c + 1)
        if c > 0:
            multiply_up(c - 1)
        send_on(c)
        if c > 1:
            combine(c - 2)
    multiply_up(last)
    combine(last - 1)
    combine(last)

    mine[...] = acc[:, width:]

    def hand_over(k):
        return pltpu.make_async_remote_copy(
            src_ref=mine,
            dst_ref=total.at[k],
            send_sem=tok_send.at[k],
            recv_sem=tok_recv.at[k],
            device_id={"section": other, "node": n, "local": (z + k) % SIDE},
            device_id_type=MESH,
        )

    for k in range(SIDE):
        hand_over(k).start()
    handed_ref[...] = acc[:, :width].astype(jnp.bfloat16)

    remote = rows_node - rows_node // NODES
    landed(out_rows.at[pl.ds(0, remote)], disp_send)
    sel_copy.wait_send()
    landed(part.at[pl.ds(0, 3)], rs_send)
    landed(grads.at[pl.ds(0, 3)], ag_send)
    landed(ret_rows, ret_send)

    for k in range(SIDE):
        hand_over(k).wait()
    sums = total[0] + total[1] + total[2] + total[3]
    for k in range(prob_ref.shape[1]):
        chosen = experts_ref[:, k : k + 1]
        wanted = (lane == chosen) | (lane == chosen + 32)
        value = jnp.sum(jnp.where(wanted, sums, 0.0), axis=1, keepdims=True)
        prob_ref[:, k : k + 1] = value.astype(jnp.bfloat16).astype(jnp.float32)


def shards(*args):
    grad_out, node_ids, expert_ids, gate_probs, gate_pre, up_pre, gate_w, up_w, down_w = args
    tokens, width = grad_out.shape
    full = width + EXTRA
    rows = gate_pre.shape[1]
    hidden = gate_pre.shape[2]
    chunks = len(CHUNKS)
    half, single = jnp.bfloat16, jnp.float32
    dma = pltpu.SemaphoreType.DMA
    in_vmem = pl.BlockSpec(memory_space=pltpu.VMEM)
    anywhere = pl.BlockSpec(memory_space=pl.ANY)
    return pl.pallas_call(
        kernel,
        out_shape=(
            jax.ShapeDtypeStruct((tokens, width), half),
            jax.ShapeDtypeStruct(gate_probs.shape, single),
        ),
        in_specs=[in_vmem] * 4 + [anywhere] * 5,
        out_specs=(in_vmem, in_vmem),
        scratch_shapes=[
            pltpu.VMEM(gate_pre.shape, half),
            pltpu.VMEM(up_pre.shape, half),
            pltpu.VMEM(gate_w.shape, half),
            pltpu.VMEM(up_w.shape, half),
            pltpu.VMEM(down_w.shape, half),
            pltpu.VMEM((tokens, full), half),
            pltpu.VMEM((rows // TILE, tokens, TILE), half),
            pltpu.VMEM((rows // TILE, tokens, TILE), half),
            pltpu.VMEM((rows, full), half),
            pltpu.VMEM((rows, full), half),
            pltpu.VMEM((4, 2, rows, hidden), half),
            pltpu.VMEM((2, rows, hidden), half),
            pltpu.VMEM((2, 2, rows, hidden), half),
            pltpu.VMEM((4, rows, SIDE * hidden), half),
            pltpu.VMEM((rows, full), half),
            pltpu.VMEM((rows, full), half),
            pltpu.VMEM((tokens, full), single),
            pltpu.VMEM((tokens, EXTRA), single),
            pltpu.VMEM((SIDE, tokens, EXTRA), single),
            dma((5,)),
            dma,
            dma((rows // TILE,)),
            dma,
            dma,
            dma,
            dma((chunks, 2)),
            dma((chunks, 2, 2)),
            dma,
            dma((chunks, 2, 2)),
            dma((chunks, 2)),
            dma,
            dma((rows // TILE,)),
            dma((SIDE,)),
            dma((SIDE,)),
        ],
        compiler_params=pltpu.CompilerParams(
            collective_id=0, has_side_effects=True, vmem_limit_bytes=62 * 1024 * 1024
        ),
    )(*args)


def solution(mesh):
    return jax.shard_map(
        shards,
        mesh=mesh,
        in_specs=(
            P(("section", "node"), "local"),
            P(("section", "node"), None),
            P(("section", "node"), None),
            P(("section", "node"), None),
            P(("section", "node"), None, "local"),
            P(("section", "node"), None, "local"),
            P(("section", "node"), "local", None),
            P(("section", "node"), "local", None),
            P(("section", "node"), None, "local"),
        ),
        out_specs=(P(("section", "node"), "local"), P(("section", "node"), None)),
        check_vma=False,
    )
```

time: 341 us -> 162 us (0.48)
  waiting for transfers between devices: 153 us -> 0 us
  Pallas kernels: 0 us -> 152 us
  blocking collectives: 106 us -> 0 us
  matrix products: 46.5 us -> 0 us
  between operations: 13.9 us -> 0.64 us
  starting transfers between devices: 11.4 us -> 0 us
  other arithmetic: 8.06 us -> 0 us
  local copies, waits for them, and re-layouts: 1.9 us -> 7.58 us
    pallas_call x0 -> x1, Pallas kernels: none -> 152 us  [shards(): pl.pallas_call(kernel, out_shape=(jax.ShapeDtypeStruct((tokens, width), h...]
    all_to_all x3 -> x0, blocking collectives: 106 us -> none  [the longest x1 51.7 us: shards(): lax.all_to_all(outgoing.reshape(node_count, capacity, slice_width), 'node...]
    psum x1 -> x0, waiting for transfers between devices: 97.1 us -> none  [shards(): lax.psum(partial_value.astype(jnp.bfloat16), 'local').astype(jnp.float32)]
    dot_general x7 -> x0, matrix products: 46.5 us -> none  [the longest x1 18.5 us: shards(): jnp.einsum('erf,edf->rd', gate_grad, gate_weight, preferred_element_type=...]
    all_gather x2 -> x0, waiting for transfers between devices: 46.4 us -> none  [the longest x1 46.4 us: shards(): lax.all_gather(up_pre, 'local', axis=2, tiled=True)]
    reduce_sum x2 -> x0, other arithmetic: 6.92 us -> none  [the longest x1 6.23 us: silu_backward(): prob_part = jnp.sum(raw_grad * active * up_value, axis=2)]
    all_to_all x1 -> x0, starting transfers between devices: 6.53 us -> none  [shards(): lax.all_to_all(prob_half.reshape(node_count, capacity, experts_here), 'no...]
    all_to_all x1 -> x0, waiting for transfers between devices: 6.32 us -> none  [shards(): lax.all_to_all(prob_half.reshape(node_count, capacity, experts_here), 'no...]
  transfers between devices with their start and end apart: 5 -> 0, of which waited for: 4 -> 0; matrix products, arithmetic and copies ran while one was open for 4% -> 0% of each run, Pallas kernels for 0% -> 0%
where the time goes in v1:
time: 162 us; the launch traced here: 160 us
  Pallas kernels  152 us (94%)
  local copies, waits for them, and re-layouts  7.58 us (5%)
    pallas_call x1, Pallas kernels, shards(): pl.pallas_call(kernel, out_shape=(jax.ShapeDtypeStruct((tokens, width), h...  152 us
    unnamed x4, local copies, waits for them, and re-layouts  6.07 us

profile of v1, /device:TPU:1, one launch (start us, length us, event | category | flops | bytes accessed | tf_op | source)
XLA Modules:
  0.0 160.1 jit_solution(11309932983535234507)
XLA Ops:
  0.6 1.4 copy.11.nodes_ref
  2.0 1.4 copy.12.experts_ref
  3.5 1.4 copy.13.probs_ref
  4.9 151.9 %shard_map.104 = (bf16[128,1792]{1,0:T(8,128)(2,1)}, f32[128,6]{1,0:T(8,128)}) custom-call(bf16[128,1792]{1,0:T(8,128)(2,1)} %x_ref.1, s32[128,4]{1,0:T(8,128)} %copy.11.nodes_ref, s32[128,6]{1,0:T(8,128)} %copy.12.experts_ref, f32[128,6]{1,0:T(8,128)} %copy.13.probs_ref, bf16[2,1024,256]{2,1,0:T(8,128)(2,1)} %gate_pre_ref.1, ...), custom_call_target="tpu_custom_call" | custom-call | tf_op jit(solution)/shard_map/pallas_call | solution.py:446
  156.8 1.5 copy.14
  158.3 1.8 %copy.16 = bf16[128,1792]{1,0:T(8,128)(2,1)} copy(bf16[128,1792]{1,0:T(8,128)(2,1)} %get-tuple-element.6) | data formatting | bytes 917504

commit v2 on v1

v2 whole, which is shorter than its diff:
```python
import functools

import jax
import jax.numpy as jnp
from jax import lax
from jax.experimental import pallas as pl
from jax.experimental.pallas import tpu as pltpu
from jax.sharding import PartitionSpec as P

MESH = pl.DeviceIdType.MESH
SIDE = 4
NODES = 16
CAP = 64
UNIT = 16
TILE = 128
BLOCK = 256
GROUP = 4
EXTRA = 128
EXPERTS = 32
CHUNKS = (8, 8, 16, 16, 8, 8)


def offset(o):
    half = o // 8
    rest = o % 8
    dy = rest // 2
    dx = (2 * (rest % 2) + dy % 2 + half) % SIDE
    return dy, dx


def nt_dot(a, b):
    return lax.dot_general(a, b, (((1,), (1,)), ((), ())), preferred_element_type=jnp.float32)


def silu_backward(raw, weight, gate, value):
    gate = gate.astype(jnp.float32)
    value = value.astype(jnp.float32)
    q = jax.nn.sigmoid(gate)
    active = gate * q
    scaled = raw * weight
    gate_grad = scaled * value * q * (1.0 + gate * (1.0 - q))
    return raw * active * value, gate_grad.astype(jnp.bfloat16), (scaled * active).astype(jnp.bfloat16)


def kernel(
    x_ref,
    nodes_ref,
    experts_ref,
    probs_ref,
    gate_pre_ref,
    up_pre_ref,
    gate_w_ref,
    up_w_ref,
    down_w_ref,
    handed_ref,
    prob_ref,
    gate_pre,
    up_pre,
    gate_w,
    up_w,
    down_w,
    table,
    x_ext,
    sel,
    sel_other,
    out_rows,
    in_rows,
    part,
    rs_far,
    rs_near,
    pre_full,
    raw_full,
    grads,
    late,
    ret_rows,
    back_rows,
    ret_prob,
    back_prob,
    acc,
    mine,
    total,
    load_sem,
    disp_send,
    disp_recv,
    sel_send,
    sel_recv,
    rs_send,
    rs_far_recv,
    rs_near_recv,
    pre_send,
    pre_recv,
    pre_far_recv,
    raw_send,
    ag_send,
    ag_recv,
    ag_far_recv,
    ret_send,
    ret_recv,
    prob_send,
    prob_recv,
    tok_send,
    tok_recv,
):
    s = lax.axis_index("section")
    n = lax.axis_index("node")
    z = lax.axis_index("local")
    other = 1 - s
    my, mx = n // SIDE, n % SIDE
    up = lax.rem(z + 1, SIDE)
    down = lax.rem(z + 3, SIDE)
    tokens, width = x_ref.shape
    rows_node = gate_pre.shape[1]
    hidden = gate_pre.shape[2]
    tiles = rows_node // TILE

    def node_plus(o):
        dy, dx = offset(o)
        return ((my + dy) % SIDE) * SIDE + (mx + dx) % SIDE

    def node_minus(o):
        dy, dx = offset(o)
        return ((my + SIDE - dy) % SIDE) * SIDE + (mx + SIDE - dx) % SIDE

    def rows_of(start, count):
        return pl.ds(start if isinstance(start, int) else pl.multiple_of(start, UNIT), count)

    def quarter(index):
        return pl.ds(pl.multiple_of(index * hidden, hidden), hidden)

    def landed(ref, sem):
        pltpu.make_async_copy(ref, ref, sem).wait()

    def send(src, dst, send_sem, recv_sem, section, node, local):
        pltpu.make_async_remote_copy(
            src_ref=src,
            dst_ref=dst,
            send_sem=send_sem,
            recv_sem=recv_sem,
            device_id={"section": section, "node": node, "local": local},
            device_id_type=MESH,
        ).start()

    def along_z(src, dst, send_sem, recv_sem, local):
        send(src, dst, send_sem, recv_sem, s, n, local)

    loads = [
        pltpu.make_async_copy(src, dst, load_sem.at[i])
        for i, (src, dst) in enumerate(
            (
                (gate_pre_ref, gate_pre),
                (up_pre_ref, up_pre),
                (down_w_ref, down_w),
                (gate_w_ref, gate_w),
                (up_w_ref, up_w),
            )
        )
    ]
    for load in loads:
        load.start()

    barrier = pltpu.get_barrier_semaphore()

    def greet(section, node, local):
        pl.semaphore_signal(
            barrier,
            inc=1,
            device_id={"section": section, "node": node, "local": local},
            device_id_type=MESH,
        )

    greet(s, n, up)
    greet(s, n, down)
    for k in range(1, SIDE):
        greet(other, n, (z + k) % SIDE)

    @pl.loop(1, NODES)
    def _(o):
        greet(s, node_plus(o), z)

    @pl.loop(0, NODES)
    def _(o):
        greet(other, node_plus(o), z)

    table[...] = jnp.zeros_like(table)
    table[0 : nodes_ref.shape[0], :] = nodes_ref[...].astype(jnp.float32)
    table[8 : 8 + experts_ref.shape[0], :] = experts_ref[...].astype(jnp.float32)
    table[16 : 16 + probs_ref.shape[0], :] = probs_ref[...]
    table[...] = table[...].T
    lane = lax.broadcasted_iota(jnp.int32, (tokens, EXTRA), 1).astype(jnp.float32)
    mass = jnp.zeros((tokens, EXTRA), jnp.float32)
    for k in range(experts_ref.shape[0]):
        mass = mass + jnp.where(
            lane == table[:, 8 + k : 9 + k], table[:, 16 + k : 17 + k], 0.0
        )
    x_ext[:, width:] = mass.astype(jnp.bfloat16)
    x_ext[:, :width] = x_ref[...]
    before = (
        lax.broadcasted_iota(jnp.int32, (tokens, tokens), 1)
        < lax.broadcasted_iota(jnp.int32, (tokens, tokens), 0)
    )
    before = jnp.where(before, 1.0, 0.0).astype(jnp.bfloat16)

    def pick(t):
        column = lax.broadcasted_iota(jnp.int32, (tokens, TILE), 1) + t * TILE
        u = column >> 4
        o = u & 15
        rest = o & 7
        dy = rest >> 1
        dx = (2 * (rest & 1) + (dy & 1) + (o >> 3)) & 3
        node = (((my + dy) & 3) * SIDE + ((mx + dx) & 3)).astype(jnp.float32)
        slot = ((u >> 4) * UNIT + (column & 15)).astype(jnp.float32)
        member = table[:, 0:1] == node
        for k in range(1, nodes_ref.shape[0]):
            member = member | (table[:, k : k + 1] == node)
        member = jnp.where(member, 1.0, 0.0)
        position = jnp.dot(
            before, member.astype(jnp.bfloat16), preferred_element_type=jnp.float32
        )
        chosen = jnp.where(position == slot, member, 0.0)
        half = t % 2 * TILE
        if not isinstance(t, int):
            half = pl.multiple_of(half, TILE)
        sel[t // 2, :, pl.ds(half, TILE)] = chosen.astype(jnp.bfloat16)
        out_rows[rows_of(t * TILE, TILE), :] = jnp.dot(
            chosen.T.astype(jnp.bfloat16), x_ext[...], preferred_element_type=jnp.float32
        ).astype(jnp.bfloat16)

    pick(0)
    pl.semaphore_wait(barrier, 2 + (SIDE - 1) + (NODES - 1) + NODES)

    starts = [UNIT * sum(CHUNKS[:c]) for c in range(len(CHUNKS))]
    sizes = [UNIT * count for count in CHUNKS]
    last = len(CHUNKS) - 1
    first_units = CHUNKS[0]

    def saved_rows(u):
        return rows_of(node_minus(u % 16) * CAP + u // 16 * UNIT, UNIT)

    def gather(ref, planes, rows, send_sem, recv_sem):
        for turn in range(2):
            for way, local in ((0, up), (1, down)):
                e = way ^ turn
                piece = ref.at[pl.ds(planes * e, planes), rows, quarter(z)]
                along_z(piece, piece, send_sem, recv_sem.at[way, e], local)

    def gather_on(ref, planes, rows, send_sem, recv_sem, far_sem):
        for way, local, owner in ((0, up, down), (1, down, up)):
            piece = ref.at[pl.ds(planes * way, planes), rows, quarter(owner)]
            landed(piece, recv_sem.at[way, way])
            along_z(piece, piece, send_sem, far_sem.at[way], local)

    def gather_near(ref, planes, rows, recv_sem):
        for way, owner in ((0, down), (1, up)):
            e = 1 - way
            landed(ref.at[pl.ds(planes * e, planes), rows, quarter(owner)], recv_sem.at[way, e])

    def gather_far(ref, planes, rows, far_sem):
        far = lax.rem(z + 2, SIDE)
        for way in range(2):
            landed(ref.at[pl.ds(planes * way, planes), rows, quarter(far)], far_sem.at[way])

    @pl.loop(0, tiles)
    def _(t):
        @pl.when(t % 2 == 0)
        def _():
            rows = rows_of(t * TILE, UNIT)
            in_rows[rows, :] = out_rows[rows, :]

        @pl.loop(1 - t % 2, TILE // UNIT)
        def _(i):
            rows = rows_of(t * TILE + i * UNIT, UNIT)
            send(
                out_rows.at[rows],
                in_rows.at[rows],
                disp_send,
                disp_recv.at[t],
                s,
                node_plus((t % 2) * 8 + i),
                z,
            )

        @pl.when(t == 0)
        def _():
            loads[0].wait()
            loads[1].wait()

            @pl.loop(0, first_units)
            def _(u):
                here, saved = rows_of(u * UNIT, UNIT), saved_rows(u)
                for e in range(2):
                    pre_full[2 * e, here, quarter(z)] = gate_pre[e, saved, :]
                    pre_full[2 * e + 1, here, quarter(z)] = up_pre[e, saved, :]

            gather(pre_full, 2, pl.ds(0, sizes[0]), pre_send, pre_recv)

        @pl.when(t + 1 < tiles)
        def _():
            pick(t + 1)

    gather_on(pre_full, 2, pl.ds(0, sizes[0]), pre_send, pre_recv, pre_far_recv)
    sel_copy = pltpu.make_async_remote_copy(
        src_ref=sel,
        dst_ref=sel_other,
        send_sem=sel_send,
        recv_sem=sel_recv,
        device_id={"section": other, "node": n, "local": z},
        device_id_type=MESH,
    )
    sel_copy.start()

    def multiply_down(c):
        begin, count = starts[c], sizes[c]
        rows = pl.ds(begin, count)
        for t in range(begin // TILE, (begin + count) // TILE):
            skip = UNIT if t % 2 == 0 else 0
            landed(in_rows.at[pl.ds(t * TILE + skip, TILE - skip)], disp_recv.at[t])
        if c == 0:
            loads[2].wait()

        def products(first, stop, step_of):
            @pl.loop(2 * first, 2 * stop)
            def _(i):
                k, e = i // 2, i % 2
                step = step_of(k)
                weights = down_w[e, quarter((z + step) % SIDE), :]
                part[k, e, rows, :] = nt_dot(in_rows[rows, :width], weights).astype(jnp.bfloat16)

        products(0, 1, lambda k: 2)
        along_z(part.at[0, 0, rows], rs_far.at[0, rows], rs_send, rs_far_recv.at[c, 0], up)
        along_z(part.at[0, 1, rows], rs_far.at[1, rows], rs_send, rs_far_recv.at[c, 1], down)
        products(1, 3, lambda k: 2 * k - 1)
        along_z(part.at[1, 1, rows], rs_near.at[0, 1, rows], rs_send, rs_near_recv.at[c, 0, 1], up)
        along_z(
            part.at[2, 0, rows], rs_near.at[1, 0, rows], rs_send, rs_near_recv.at[c, 1, 0], down
        )
        products(3, 4, lambda k: 0)

    def add_far(c):
        rows = pl.ds(starts[c], sizes[c])
        for way, local in ((0, up), (1, down)):
            landed(rs_far.at[way, rows], rs_far_recv.at[c, way])
            part[1 + way, way, rows, :] = (
                part[1 + way, way, rows, :].astype(jnp.float32)
                + rs_far[way, rows, :].astype(jnp.float32)
            ).astype(jnp.bfloat16)
            along_z(
                part.at[1 + way, way, rows],
                rs_near.at[way, way, rows],
                rs_send,
                rs_near_recv.at[c, way, way],
                local,
            )

    def expert_weight(here, e):
        masses = in_rows[here, width:].astype(jnp.float32)
        expert = lax.broadcasted_iota(jnp.int32, masses.shape, 1)
        return jnp.sum(jnp.where(expert == 2 * n + e, masses, 0.0), axis=1, keepdims=True)

    def hidden_grads(c):
        begin, count = starts[c], sizes[c]
        rows = pl.ds(begin, count)
        for way in range(2):
            for e in range(2):
                landed(rs_near.at[way, e, rows], rs_near_recv.at[c, way, e])
        step = GROUP * UNIT

        @pl.loop(begin // step, (begin + count) // step)
        def _(g):
            here = rows_of(g * step, step)
            expert = lax.broadcasted_iota(jnp.int32, (step, EXTRA), 1)
            extra = jnp.zeros((step, EXTRA), jnp.float32)
            saved = [saved_rows(g * GROUP + i) for i in range(GROUP)]
            for e in range(2):
                raw = (
                    part[3, e, here, :].astype(jnp.float32)
                    + rs_near[0, e, here, :].astype(jnp.float32)
                    + rs_near[1, e, here, :].astype(jnp.float32)
                )
                terms, gate_grad, up_grad = silu_backward(
                    raw,
                    expert_weight(here, e),
                    jnp.concatenate([gate_pre[e, one, :] for one in saved], axis=0),
                    jnp.concatenate([up_pre[e, one, :] for one in saved], axis=0),
                )
                prob = jnp.sum(terms, axis=1, keepdims=True)
                high = prob.astype(jnp.bfloat16).astype(jnp.float32)
                extra = jnp.where(expert == 2 * n + e, high, extra)
                extra = jnp.where(expert == EXPERTS + 2 * n + e, prob - high, extra)
                grads[2 * e, here, quarter(z)] = gate_grad
                grads[2 * e + 1, here, quarter(z)] = up_grad
                if c == 0:
                    raw_full[e, here, quarter(z)] = raw.astype(jnp.bfloat16)
            ret_prob[here, :] = extra.astype(jnp.bfloat16)

        if c == 0:
            gather(raw_full, 1, rows, raw_send, ag_recv.at[c])
        else:
            gather(grads, 2, rows, ag_send, ag_recv.at[c])

        @pl.loop(begin // UNIT, (begin + count) // UNIT)
        def _(u):
            here = rows_of(u * UNIT, UNIT)
            send(
                ret_prob.at[here],
                back_prob.at[here],
                prob_send,
                prob_recv,
                other,
                node_minus(u % 16),
                z,
            )

    def send_on(c):
        rows = pl.ds(starts[c], sizes[c])
        if c == 0:
            gather_on(raw_full, 1, rows, raw_send, ag_recv.at[c], ag_far_recv.at[c])
        else:
            gather_on(grads, 2, rows, ag_send, ag_recv.at[c], ag_far_recv.at[c])

    def send_back(c, features):
        @pl.loop(starts[c] // UNIT, (starts[c] + sizes[c]) // UNIT)
        def _(u):
            here = rows_of(u * UNIT, UNIT)
            send(
                ret_rows.at[here, features],
                back_rows.at[here, features],
                ret_send,
                ret_recv.at[u // 16],
                other,
                node_minus(u % 16),
                z,
            )

    def feature_tile(i):
        return pl.ds(pl.multiple_of(i * 256, 256), 256)

    def up_product(rows, features, columns):
        return (
            nt_dot(grads[0, rows, columns], gate_w[0, features, columns])
            + nt_dot(grads[1, rows, columns], up_w[0, features, columns])
            + nt_dot(grads[2, rows, columns], gate_w[1, features, columns])
            + nt_dot(grads[3, rows, columns], up_w[1, features, columns])
        )

    def multiply_up(c):
        rows = pl.ds(starts[c], sizes[c])
        if c == 0:
            gather_near(raw_full, 1, rows, ag_recv.at[c])
            gather_far(raw_full, 1, rows, ag_far_recv.at[c])
            gather_near(pre_full, 2, rows, pre_recv)
            gather_far(pre_full, 2, rows, pre_far_recv)
            step = GROUP * UNIT
            groups = sizes[0] // step

            @pl.loop(0, (SIDE - 1) * groups)
            def _(i):
                here = rows_of(i % groups * step, step)
                columns = quarter((z + 1 + i // groups) % SIDE)
                for e in range(2):
                    _, gate_grad, up_grad = silu_backward(
                        raw_full[e, here, columns].astype(jnp.float32),
                        expert_weight(here, e),
                        pre_full[2 * e, here, columns],
                        pre_full[2 * e + 1, here, columns],
                    )
                    grads[2 * e, here, columns] = gate_grad
                    grads[2 * e + 1, here, columns] = up_grad

            loads[3].wait()
            loads[4].wait()
        else:
            gather_near(grads, 2, rows, ag_recv.at[c])
            gather_far(grads, 2, rows, ag_far_recv.at[c])

        @pl.loop(0, width // 256)
        def _(i):
            features = feature_tile(i)
            ret_rows[rows, features] = up_product(rows, features, pl.ds(0, SIDE * hidden)).astype(
                jnp.bfloat16
            )

        send_back(c, pl.ds(0, width))

    def multiply_up_near(c):
        rows = pl.ds(starts[c], sizes[c])
        gather_near(grads, 2, rows, ag_recv.at[c])

        @pl.loop(0, width // 256)
        def _(i):
            features = feature_tile(i)
            late[:, features] = (
                up_product(rows, features, quarter(z))
                + up_product(rows, features, quarter(up))
                + up_product(rows, features, quarter(down))
            )

    def multiply_up_far(c):
        rows = pl.ds(starts[c], sizes[c])
        gather_far(grads, 2, rows, ag_far_recv.at[c])
        columns = quarter(lax.rem(z + 2, SIDE))
        cut = width // 256 // 2 + 1
        for first, stop in ((0, cut), (cut, width // 256)):

            @pl.loop(first, stop)
            def _(i):
                features = feature_tile(i)
                ret_rows[rows, features] = (
                    late[:, features] + up_product(rows, features, columns)
                ).astype(jnp.bfloat16)

            send_back(c, pl.ds(first * 256, (stop - first) * 256))

    def combine(b):
        rows = pl.ds(b * BLOCK, BLOCK)
        landed(back_rows.at[rows], ret_recv.at[b])

        @pl.loop(0, width // 256)
        def _(i):
            features = feature_tile(i)
            term = jnp.dot(
                sel_other[b], back_rows[rows, features], preferred_element_type=jnp.float32
            )
            if b == 0:
                acc[:, features] = term
            elif b < rows_node // BLOCK - 1:
                acc[:, features] += term
            else:
                handed_ref[:, features] = (acc[:, features] + term).astype(jnp.bfloat16)

    def hand_over(k):
        return pltpu.make_async_remote_copy(
            src_ref=mine,
            dst_ref=total.at[k],
            send_sem=tok_send.at[k],
            recv_sem=tok_recv.at[k],
            device_id={"section": other, "node": n, "local": (z + k) % SIDE},
            device_id_type=MESH,
        )

    multiply_down(0)
    add_far(0)
    hidden_grads(0)
    multiply_down(1)
    send_on(0)
    add_far(1)
    for c in range(1, last + 1):
        if c < last:
            multiply_down(c + 1)
        hidden_grads(c)
        if c < last:
            add_far(c + 1)
        multiply_up(c - 1)
        send_on(c)
        if c == 4:
            sel_copy.wait_recv()
            combine(0)
        if c == 5:
            combine(1)
    multiply_up_near(last)
    landed(back_prob, prob_recv)
    tokens_prob = jnp.zeros((tokens, EXTRA), jnp.float32)
    for b in range(rows_node // BLOCK):
        tokens_prob = tokens_prob + jnp.dot(
            sel_other[b],
            back_prob[b * BLOCK : (b + 1) * BLOCK, :],
            preferred_element_type=jnp.float32,
        )
    mine[...] = tokens_prob
    for k in range(SIDE):
        hand_over(k).start()
    combine(2)
    multiply_up_far(last)

    for k in range(SIDE):
        hand_over(k).wait()
    sums = (total[0] + total[1] + total[2] + total[3]).T
    sums = sums[:EXPERTS] + sums[EXPERTS : 2 * EXPERTS]
    expert = lax.broadcasted_iota(jnp.int32, (EXPERTS, tokens), 0)
    for k in range(prob_ref.shape[0]):
        value = jnp.sum(
            jnp.where(expert == experts_ref[k : k + 1, :], sums, 0.0), axis=0, keepdims=True
        )
        prob_ref[k : k + 1, :] = value.astype(jnp.bfloat16).astype(jnp.float32)

    landed(out_rows.at[pl.ds(0, rows_node - rows_node // NODES)], disp_send)
    sel_copy.wait_send()
    landed(part.at[pl.ds(0, 3)], rs_send)
    landed(pre_full.at[pl.ds(0, 3)], pre_send)
    landed(raw_full.at[:, :, pl.ds(0, 3 * hidden)], raw_send)
    landed(grads.at[pl.ds(0, 3), pl.ds(0, rows_node - sizes[0])], ag_send)
    landed(ret_prob, prob_send)
    landed(ret_rows, ret_send)
    combine(3)


def shards(*args):
    grad_out, node_ids, expert_ids, gate_probs, gate_pre, up_pre, gate_w, up_w, down_w = args
    tokens, width = grad_out.shape
    full = width + EXTRA
    rows = gate_pre.shape[1]
    hidden = gate_pre.shape[2]
    chunks = len(CHUNKS)
    first = UNIT * CHUNKS[0]
    half, single = jnp.bfloat16, jnp.float32
    dma = pltpu.SemaphoreType.DMA
    in_vmem = pl.BlockSpec(memory_space=pltpu.VMEM)
    anywhere = pl.BlockSpec(memory_space=pl.ANY)
    results = (
        pltpu.VMEM((tokens, width), half),
        pltpu.VMEM(gate_probs.shape[::-1], single),
    )
    handed, prob = pl.pallas_call(
        kernel,
        out_shape=results,
        in_specs=[in_vmem] * 4 + [anywhere] * 5,
        out_specs=(in_vmem, in_vmem),
        scratch_shapes=[
            pltpu.VMEM(gate_pre.shape, half),
            pltpu.VMEM(up_pre.shape, half),
            pltpu.VMEM(gate_w.shape, half),
            pltpu.VMEM(up_w.shape, half),
            pltpu.VMEM(down_w.shape, half),
            pltpu.VMEM((tokens, tokens), single),
            pltpu.VMEM((tokens, full), half),
            pltpu.VMEM((rows // BLOCK, tokens, BLOCK), half),
            pltpu.VMEM((rows // BLOCK, tokens, BLOCK), half),
            pltpu.VMEM((rows, full), half),
            pltpu.VMEM((rows, full), half),
            pltpu.VMEM((4, 2, rows, hidden), half),
            pltpu.VMEM((2, rows, hidden), half),
            pltpu.VMEM((2, 2, rows, hidden), half),
            pltpu.VMEM((4, first, SIDE * hidden), half),
            pltpu.VMEM((2, first, SIDE * hidden), half),
            pltpu.VMEM((4, rows, SIDE * hidden), half),
            pltpu.VMEM((UNIT * CHUNKS[-1], width), single),
            pltpu.VMEM((rows, width), half),
            pltpu.VMEM((rows, width), half),
            pltpu.VMEM((rows, EXTRA), half),
            pltpu.VMEM((rows, EXTRA), half),
            pltpu.VMEM((tokens, width), single),
            pltpu.VMEM((tokens, EXTRA), single),
            pltpu.VMEM((SIDE, tokens, EXTRA), single),
            dma((5,)),
            dma,
            dma((rows // TILE,)),
            dma,
            dma,
            dma,
            dma((chunks, 2)),
            dma((chunks, 2, 2)),
            dma,
            dma((2, 2)),
            dma((2,)),
            dma,
            dma,
            dma((chunks, 2, 2)),
            dma((chunks, 2)),
            dma,
            dma((rows // BLOCK,)),
            dma,
            dma,
            dma((SIDE,)),
            dma((SIDE,)),
        ],
        compiler_params=pltpu.CompilerParams(
            collective_id=0, has_side_effects=True, vmem_limit_bytes=62 * 1024 * 1024
        ),
    )(
        grad_out,
        node_ids.T,
        expert_ids.T,
        gate_probs.T,
        gate_pre,
        up_pre,
        gate_w,
        up_w,
        down_w,
    )
    return handed, prob.T


def solution(mesh):
    return jax.shard_map(
        shards,
        mesh=mesh,
        in_specs=(
            P(("section", "node"), "local"),
            P(("section", "node"), None),
            P(("section", "node"), None),
            P(("section", "node"), None),
            P(("section", "node"), None, "local"),
            P(("section", "node"), None, "local"),
            P(("section", "node"), "local", None),
            P(("section", "node"), "local", None),
            P(("section", "node"), None, "local"),
        ),
        out_specs=(P(("section", "node"), "local"), P(("section", "node"), None)),
        check_vma=False,
    )
```

time: 162 us -> 144 us (0.89); the launches traced: 160 us -> 144 us
  Pallas kernels: 152 us -> 142 us
  local copies, waits for them, and re-layouts: 7.58 us -> 1.36 us
    pallas_call x1, Pallas kernels: 152 us -> 142 us  [shards(): pl.pallas_call(kernel, out_shape=results, in_specs=[in_vmem] * 4 + [anywh...]
    unnamed x4 -> x2, local copies, waits for them, and re-layouts: 6.07 us -> 1.36 us
where the time goes in v2:
time: 144 us
  Pallas kernels  142 us (99%)
    pallas_call x1, Pallas kernels, shards(): pl.pallas_call(kernel, out_shape=results, in_specs=[in_vmem] * 4 + [anywh...  142 us

profile of v2, /device:TPU:1, one launch (start us, length us, event | category | flops | bytes accessed | tf_op | source)
XLA Modules:
  0.0 144.1 jit_solution(9605739193988897387)
XLA Ops:
  0.6 142.1 %shard_map.104 = (bf16[128,1792]{1,0:T(8,128)(2,1)S(1)}, f32[6,128]{1,0:T(8,128)S(1)}) custom-call(bf16[128,1792]{1,0:T(8,128)(2,1)} %x_ref.1, s32[4,128]{1,0:T(4,128)} %bitcast.7, s32[6,128]{1,0:T(8,128)} %bitcast.5, f32[6,128]{1,0:T(8,128)} %bitcast.6, bf16[2,1024,256]{2,1,0:T(8,128)(2,1)} %gate_pre_ref.1, bf16[2,1024,256]{2,1,0:T(8,128)(2,1)} %up_pre_ref.1, ...), custom_call_target="tpu_custom_call" | custom-call | tf_op jit(solution)/shard_map/pallas_call | solution.py:612
  142.8 0.8 copy.13
  143.5 0.6 copy.14

commit v3 on v2

--- a/solution.py
+++ b/solution.py
@@ -1,5 +1,3 @@
-import functools
-
 import jax
 import jax.numpy as jnp
 from jax import lax
@@ -17,15 +15,38 @@
 GROUP = 4
 EXTRA = 128
 EXPERTS = 32
-CHUNKS = (8, 8, 16, 16, 8, 8)
-
-
-def offset(o):
-    half = o // 8
-    rest = o % 8
-    dy = rest // 2
-    dx = (2 * (rest % 2) + dy % 2 + half) % SIDE
-    return dy, dx
+CHUNKS = (8, 8, 8, 8, 8, 8, 8, 8)
+
+
+def near(u):
+    i = u % 4
+    return u // 4 % 4, i // 2 * (1 + 2 * (i % 2)), (1 - i // 2) * (1 + 2 * (i % 2))
+
+
+def near_last(u):
+    return 3, *near(u)[1:]
+
+
+def straight(u):
+    return (u - 12) // 2, 2 * (u % 2), 2 * (1 - u % 2)
+
+
+def diagonal(u):
+    place = 4 * ((u - 20) % 9) % 9
+    return (u - 20) // 9, 1 + place // 3, 1 + place % 3
+
+
+def home(u):
+    return u - 60, 0, 0
+
+
+RANGES = ((0, 12, near), (12, 20, straight), (20, 56, diagonal), (56, 60, near_last), (60, 64, home))
+
+
+def ranges(begin, stop):
+    for low, high, place in RANGES:
+        if max(begin, low) < min(stop, high):
+            yield max(begin, low), min(stop, high), place
 
 
 def nt_dot(a, b):
@@ -60,6 +81,8 @@
     up_w,
     down_w,
     table,
+    column_node,
+    column_slot,
     x_ext,
     sel,
     sel_other,
@@ -113,12 +136,10 @@
     hidden = gate_pre.shape[2]
     tiles = rows_node // TILE
 
-    def node_plus(o):
-        dy, dx = offset(o)
+    def node_plus(dy, dx):
         return ((my + dy) % SIDE) * SIDE + (mx + dx) % SIDE
 
-    def node_minus(o):
-        dy, dx = offset(o)
+    def node_minus(dy, dx):
         return ((my + SIDE - dy) % SIDE) * SIDE + (mx + SIDE - dx) % SIDE
 
     def rows_of(start, count):
@@ -175,11 +196,11 @@
 
     @pl.loop(1, NODES)
     def _(o):
-        greet(s, node_plus(o), z)
+        greet(s, node_plus(o // SIDE, o % SIDE), z)
 
     @pl.loop(0, NODES)
     def _(o):
-        greet(other, node_plus(o), z)
+        greet(other, node_plus(o // SIDE, o % SIDE), z)
 
     table[...] = jnp.zeros_like(table)
     table[0 : nodes_ref.shape[0], :] = nodes_ref[...].astype(jnp.float32)
@@ -200,15 +221,22 @@
     )
     before = jnp.where(before, 1.0, 0.0).astype(jnp.bfloat16)
 
+    unit_of_lane = lax.broadcasted_iota(jnp.int32, (1, TILE), 1) // UNIT
+    slot_of_lane = lax.broadcasted_iota(jnp.int32, (1, TILE), 1) % UNIT
+    for t in range(tiles):
+        node = jnp.zeros((1, TILE), jnp.int32)
+        slot = slot_of_lane
+        for i in range(TILE // UNIT):
+            u = t * (TILE // UNIT) + i
+            place = next(f for low, high, f in RANGES if low <= u < high)
+            q, dy, dx = place(u)
+            node = jnp.where(unit_of_lane == i, node_plus(dy, dx), node)
+            slot = slot + jnp.where(unit_of_lane == i, q * UNIT, 0)
+        column_node[t : t + 1, :] = node.astype(jnp.float32)
+        column_slot[t : t + 1, :] = slot.astype(jnp.float32)
+
     def pick(t):
-        column = lax.broadcasted_iota(jnp.int32, (tokens, TILE), 1) + t * TILE
-        u = column >> 4
-        o = u & 15
-        rest = o & 7
-        dy = rest >> 1
-        dx = (2 * (rest & 1) + (dy & 1) + (o >> 3)) & 3
-        node = (((my + dy) & 3) * SIDE + ((mx + dx) & 3)).astype(jnp.float32)
-        slot = ((u >> 4) * UNIT + (column & 15)).astype(jnp.float32)
+        node = column_node[t : t + 1, :]
         member = table[:, 0:1] == node
         for k in range(1, nodes_ref.shape[0]):
             member = member | (table[:, k : k + 1] == node)
@@ -216,14 +244,16 @@
         position = jnp.dot(
             before, member.astype(jnp.bfloat16), preferred_element_type=jnp.float32
         )
-        chosen = jnp.where(position == slot, member, 0.0)
-        half = t % 2 * TILE
-        if not isinstance(t, int):
-            half = pl.multiple_of(half, TILE)
-        sel[t // 2, :, pl.ds(half, TILE)] = chosen.astype(jnp.bfloat16)
-        out_rows[rows_of(t * TILE, TILE), :] = jnp.dot(
-            chosen.T.astype(jnp.bfloat16), x_ext[...], preferred_element_type=jnp.float32
-        ).astype(jnp.bfloat16)
+        chosen = jnp.where(position == column_slot[t : t + 1, :], member, 0.0)
+        sel[t // 2, :, t % 2 * TILE : (t % 2 + 1) * TILE] = chosen.astype(jnp.bfloat16)
+        picked = chosen.T.astype(jnp.bfloat16)
+
+        @pl.loop(0, x_ext.shape[1] // 384)
+        def _(i):
+            features = pl.ds(pl.multiple_of(i * 384, 128), 384)
+            out_rows[t * TILE : (t + 1) * TILE, features] = jnp.dot(
+                picked, x_ext[:, features], preferred_element_type=jnp.float32
+            ).astype(jnp.bfloat16)
 
     pick(0)
     pl.semaphore_wait(barrier, 2 + (SIDE - 1) + (NODES - 1) + NODES)
@@ -233,8 +263,8 @@
     last = len(CHUNKS) - 1
     first_units = CHUNKS[0]
 
-    def saved_rows(u):
-        return rows_of(node_minus(u % 16) * CAP + u // 16 * UNIT, UNIT)
+    def saved_rows(q, dy, dx):
+        return rows_of(node_minus(dy, dx) * CAP + q * UNIT, UNIT)
 
     def gather(ref, planes, rows, send_sem, recv_sem):
         for turn in range(2):
@@ -259,61 +289,72 @@
         for way in range(2):
             landed(ref.at[pl.ds(planes * way, planes), rows, quarter(far)], far_sem.at[way])
 
-    @pl.loop(0, tiles)
-    def _(t):
-        @pl.when(t % 2 == 0)
-        def _():
-            rows = rows_of(t * TILE, UNIT)
-            in_rows[rows, :] = out_rows[rows, :]
-
-        @pl.loop(1 - t % 2, TILE // UNIT)
-        def _(i):
-            rows = rows_of(t * TILE + i * UNIT, UNIT)
-            send(
-                out_rows.at[rows],
-                in_rows.at[rows],
-                disp_send,
-                disp_recv.at[t],
-                s,
-                node_plus((t % 2) * 8 + i),
-                z,
-            )
-
-        @pl.when(t == 0)
-        def _():
-            loads[0].wait()
-            loads[1].wait()
-
-            @pl.loop(0, first_units)
+    def send_rows(t):
+        if t > 0:
+            pick(t)
+        for low, high, place in ranges(t * TILE // UNIT, (t + 1) * TILE // UNIT):
+            if place is home:
+                rows = pl.ds(low * UNIT, (high - low) * UNIT)
+                in_rows[rows, :] = out_rows[rows, :]
+                continue
+
+            @pl.loop(low, high)
             def _(u):
-                here, saved = rows_of(u * UNIT, UNIT), saved_rows(u)
+                rows = rows_of(u * UNIT, UNIT)
+                _, dy, dx = place(u)
+                send(
+                    out_rows.at[rows],
+                    in_rows.at[rows],
+                    disp_send,
+                    disp_recv.at[t],
+                    s,
+                    node_plus(dy, dx),
+                    z,
+                )
+
+        if t == tiles - 1:
+            sel_copy().start()
+
+    def rows_arrived(t):
+        remote = sum(
+            high - low
+            for low, high, place in ranges(t * TILE // UNIT, (t + 1) * TILE // UNIT)
+            if place is not home
+        )
+        landed(in_rows.at[pl.ds(t * TILE, remote * UNIT)], disp_recv.at[t])
+
+    def sel_copy():
+        return pltpu.make_async_remote_copy(
+            src_ref=sel,
+            dst_ref=sel_other,
+            send_sem=sel_send,
+            recv_sem=sel_recv,
+            device_id={"section": other, "node": n, "local": z},
+            device_id_type=MESH,
+        )
+
+    def gather_saved(_):
+        loads[0].wait()
+        loads[1].wait()
+        for low, high, place in ranges(0, first_units):
+
+            @pl.loop(low, high)
+            def _(u):
+                here, saved = rows_of(u * UNIT, UNIT), saved_rows(*place(u))
                 for e in range(2):
                     pre_full[2 * e, here, quarter(z)] = gate_pre[e, saved, :]
                     pre_full[2 * e + 1, here, quarter(z)] = up_pre[e, saved, :]
 
-            gather(pre_full, 2, pl.ds(0, sizes[0]), pre_send, pre_recv)
-
-        @pl.when(t + 1 < tiles)
-        def _():
-            pick(t + 1)
-
-    gather_on(pre_full, 2, pl.ds(0, sizes[0]), pre_send, pre_recv, pre_far_recv)
-    sel_copy = pltpu.make_async_remote_copy(
-        src_ref=sel,
-        dst_ref=sel_other,
-        send_sem=sel_send,
-        recv_sem=sel_recv,
-        device_id={"section": other, "node": n, "local": z},
-        device_id_type=MESH,
-    )
-    sel_copy.start()
+        gather(pre_full, 2, pl.ds(0, sizes[0]), pre_send, pre_recv)
+
+    def gather_saved_on(_):
+        gather_on(pre_full, 2, pl.ds(0, sizes[0]), pre_send, pre_recv, pre_far_recv)
 
     def multiply_down(c):
         begin, count = starts[c], sizes[c]
         rows = pl.ds(begin, count)
         for t in range(begin // TILE, (begin + count) // TILE):
-            skip = UNIT if t % 2 == 0 else 0
-            landed(in_rows.at[pl.ds(t * TILE + skip, TILE - skip)], disp_recv.at[t])
+            rows_arrived(t)
         if c == 0:
             loads[2].wait()
 
@@ -364,12 +405,11 @@
                 landed(rs_near.at[way, e, rows], rs_near_recv.at[c, way, e])
         step = GROUP * UNIT
 
-        @pl.loop(begin // step, (begin + count) // step)
-        def _(g):
+        def one_group(g, place):
             here = rows_of(g * step, step)
             expert = lax.broadcasted_iota(jnp.int32, (step, EXTRA), 1)
             extra = jnp.zeros((step, EXTRA), jnp.float32)
-            saved = [saved_rows(g * GROUP + i) for i in range(GROUP)]
+            saved = [saved_rows(*place(g * GROUP + i)) for i in range(GROUP)]
             for e in range(2):
                 raw = (
                     part[3, e, here, :].astype(jnp.float32)
@@ -392,23 +432,32 @@
                     raw_full[e, here, quarter(z)] = raw.astype(jnp.bfloat16)
             ret_prob[here, :] = extra.astype(jnp.bfloat16)
 
+        for low, high, place in ranges(begin // UNIT, (begin + count) // UNIT):
+
+            @pl.loop(low // GROUP, high // GROUP)
+            def _(g):
+                one_group(g, place)
+
         if c == 0:
             gather(raw_full, 1, rows, raw_send, ag_recv.at[c])
         else:
             gather(grads, 2, rows, ag_send, ag_recv.at[c])
 
-        @pl.loop(begin // UNIT, (begin + count) // UNIT)
-        def _(u):
-            here = rows_of(u * UNIT, UNIT)
-            send(
-                ret_prob.at[here],
-                back_prob.at[here],
-                prob_send,
-                prob_recv,
-                other,
-                node_minus(u % 16),
-                z,
-            )
+        for low, high, place in ranges(begin // UNIT, (begin + count) // UNIT):
+
+            @pl.loop(low, high)
+            def _(u):
+                here = rows_of(u * UNIT, UNIT)
+                _, dy, dx = place(u)
+                send(
+                    ret_prob.at[here],
+                    back_prob.at[here],
+                    prob_send,
+                    prob_recv,
+                    other,
+                    node_minus(dy, dx),
+                    z,
+                )
 
     def send_on(c):
         rows = pl.ds(starts[c], sizes[c])
@@ -418,18 +467,21 @@
             gather_on(grads, 2, rows, ag_send, ag_recv.at[c], ag_far_recv.at[c])
 
     def send_back(c, features):
-        @pl.loop(starts[c] // UNIT, (starts[c] + sizes[c]) // UNIT)
-        def _(u):
-            here = rows_of(u * UNIT, UNIT)
-            send(
-                ret_rows.at[here, features],
-                back_rows.at[here, features],
-                ret_send,
-                ret_recv.at[u // 16],
-                other,
-                node_minus(u % 16),
-                z,
-            )
+        for low, high, place in ranges(starts[c] // UNIT, (starts[c] + sizes[c]) // UNIT):
+
+            @pl.loop(low, high)
+            def _(u):
+                here = rows_of(u * UNIT, UNIT)
+                _, dy, dx = place(u)
+                send(
+                    ret_rows.at[here, features],
+                    back_rows.at[here, features],
+                    ret_send,
+                    ret_recv.at[u // 16],
+                    other,
+                    node_minus(dy, dx),
+                    z,
+                )
 
     def feature_tile(i):
         return pl.ds(pl.multiple_of(i * 256, 256), 256)
@@ -442,7 +494,7 @@
             + nt_dot(grads[3, rows, columns], up_w[1, features, columns])
         )
 
-    def multiply_up(c):
+    def await_grads(c):
         rows = pl.ds(starts[c], sizes[c])
         if c == 0:
             gather_near(raw_full, 1, rows, ag_recv.at[c])
@@ -472,14 +524,34 @@
             gather_near(grads, 2, rows, ag_recv.at[c])
             gather_far(grads, 2, rows, ag_far_recv.at[c])
 
-        @pl.loop(0, width // 256)
+    cut = width // 256 // 2 + 1
+
+    def multiply_up(c, first, stop):
+        rows = pl.ds(starts[c], sizes[c])
+
+        @pl.loop(first, stop)
         def _(i):
             features = feature_tile(i)
             ret_rows[rows, features] = up_product(rows, features, pl.ds(0, SIDE * hidden)).astype(
                 jnp.bfloat16
             )
 
-        send_back(c, pl.ds(0, width))
+        send_back(c, pl.ds(first * 256, (stop - first) * 256))
+
+    def multiply_up_low(c):
+        await_grads(c)
+        multiply_up(c, 0, cut)
+
+    def multiply_up_high(c):
+        multiply_up(c, cut, width // 256)
+
+    def multiply_up_own(c):
+        rows = pl.ds(starts[c], sizes[c])
+
+        @pl.loop(0, width // 256)
+        def _(i):
+            features = feature_tile(i)
+            late[:, features] = up_product(rows, features, quarter(z))
 
     def multiply_up_near(c):
         rows = pl.ds(starts[c], sizes[c])
@@ -488,17 +560,14 @@
         @pl.loop(0, width // 256)
         def _(i):
             features = feature_tile(i)
-            late[:, features] = (
-                up_product(rows, features, quarter(z))
-                + up_product(rows, features, quarter(up))
-                + up_product(rows, features, quarter(down))
+            late[:, features] += up_product(rows, features, quarter(up)) + up_product(
+                rows, features, quarter(down)
             )
 
     def multiply_up_far(c):
         rows = pl.ds(starts[c], sizes[c])
         gather_far(grads, 2, rows, ag_far_recv.at[c])
         columns = quarter(lax.rem(z + 2, SIDE))
-        cut = width // 256 // 2 + 1
         for first, stop in ((0, cut), (cut, width // 256)):
 
             @pl.loop(first, stop)
@@ -512,6 +581,8 @@
 
     def combine(b):
         rows = pl.ds(b * BLOCK, BLOCK)
+        if b == 0:
+            sel_copy().wait_recv()
         landed(back_rows.at[rows], ret_recv.at[b])
 
         @pl.loop(0, width // 256)
@@ -537,39 +608,85 @@
             device_id_type=MESH,
         )
 
-    multiply_down(0)
-    add_far(0)
-    hidden_grads(0)
-    multiply_down(1)
-    send_on(0)
-    add_far(1)
-    for c in range(1, last + 1):
-        if c < last:
-            multiply_down(c + 1)
-        hidden_grads(c)
-        if c < last:
-            add_far(c + 1)
-        multiply_up(c - 1)
-        send_on(c)
-        if c == 4:
-            sel_copy.wait_recv()
-            combine(0)
-        if c == 5:
-            combine(1)
-    multiply_up_near(last)
-    landed(back_prob, prob_recv)
-    tokens_prob = jnp.zeros((tokens, EXTRA), jnp.float32)
-    for b in range(rows_node // BLOCK):
-        tokens_prob = tokens_prob + jnp.dot(
-            sel_other[b],
-            back_prob[b * BLOCK : (b + 1) * BLOCK, :],
-            preferred_element_type=jnp.float32,
-        )
-    mine[...] = tokens_prob
-    for k in range(SIDE):
-        hand_over(k).start()
-    combine(2)
-    multiply_up_far(last)
+    def sum_prob(_):
+        landed(back_prob, prob_recv)
+        tokens_prob = jnp.zeros((tokens, EXTRA), jnp.float32)
+        for b in range(rows_node // BLOCK):
+            tokens_prob = tokens_prob + jnp.dot(
+                sel_other[b],
+                back_prob[b * BLOCK : (b + 1) * BLOCK, :],
+                preferred_element_type=jnp.float32,
+            )
+        mine[...] = tokens_prob
+        for k in range(SIDE):
+            hand_over(k).start()
+
+    for step, index in (
+        (send_rows, 0),
+        (gather_saved, 0),
+        (send_rows, 1),
+        (send_rows, 2),
+        (send_rows, 3),
+        (send_rows, 4),
+        (multiply_down, 0),
+        (gather_saved_on, 0),
+        (add_far, 0),
+        (multiply_down, 1),
+        (send_rows, 5),
+        (hidden_grads, 0),
+        (multiply_down, 2),
+        (add_far, 1),
+        (send_on, 0),
+        (multiply_down, 3),
+        (hidden_grads, 1),
+        (add_far, 2),
+        (multiply_up_low, 0),
+        (add_far, 3),
+        (send_on, 1),
+        (multiply_down, 4),
+        (hidden_grads, 2),
+        (multiply_down, 5),
+        (send_rows, 6),
+        (multiply_up_high, 0),
+        (add_far, 4),
+        (send_on, 2),
+        (hidden_grads, 3),
+        (send_rows, 7),
+        (multiply_up_low, 1),
+        (multiply_up_high, 1),
+        (hidden_grads, 4),
+        (add_far, 5),
+        (multiply_up_low, 2),
+        (send_on, 3),
+        (multiply_down, 6),
+        (multiply_down, 7),
+        (multiply_up_high, 2),
+        (send_on, 4),
+        (hidden_grads, 5),
+        (multiply_up_low, 3),
+        (multiply_up_high, 3),
+        (add_far, 6),
+        (multiply_up_low, 4),
+        (send_on, 5),
+        (add_far, 7),
+        (multiply_up_high, 4),
+        (hidden_grads, 6),
+        (combine, 0),
+        (multiply_up_low, 5),
+        (send_on, 6),
+        (hidden_grads, 7),
+        (multiply_up_own, 7),
+        (multiply_up_high, 5),
+        (multiply_up_low, 6),
+        (send_on, 7),
+        (multiply_up_high, 6),
+        (multiply_up_near, 7),
+        (sum_prob, 0),
+        (multiply_up_far, 7),
+        (combine, 1),
+        (combine, 2),
+    ):
+        step(index)
 
     for k in range(SIDE):
         hand_over(k).wait()
@@ -583,7 +700,7 @@
         prob_ref[k : k + 1, :] = value.astype(jnp.bfloat16).astype(jnp.float32)
 
     landed(out_rows.at[pl.ds(0, rows_node - rows_node // NODES)], disp_send)
-    sel_copy.wait_send()
+    sel_copy().wait_send()
     landed(part.at[pl.ds(0, 3)], rs_send)
     landed(pre_full.at[pl.ds(0, 3)], pre_send)
     landed(raw_full.at[:, :, pl.ds(0, 3 * hidden)], raw_send)
@@ -621,6 +738,8 @@
             pltpu.VMEM(up_w.shape, half),
             pltpu.VMEM(down_w.shape, half),
             pltpu.VMEM((tokens, tokens), single),
+            pltpu.VMEM((rows // TILE, TILE), single),
+            pltpu.VMEM((rows // TILE, TILE), single),
             pltpu.VMEM((tokens, full), half),
             pltpu.VMEM((rows // BLOCK, tokens, BLOCK), half),
             pltpu.VMEM((rows // BLOCK, tokens, BLOCK), half),

time: 144 us -> 134 us (0.931)
  Pallas kernels: 142 us -> 132 us
    pallas_call x1, Pallas kernels: 142 us -> 132 us  [shards(): pl.pallas_call(kernel, out_shape=results, in_specs=[in_vmem] * 4 + [anywh...]
where the time goes in v3:
time: 134 us
  Pallas kernels  132 us (99%)
  local copies, waits for them, and re-layouts  1.36 us (1%)
    pallas_call x1, Pallas kernels, shards(): pl.pallas_call(kernel, out_shape=results, in_specs=[in_vmem] * 4 + [anywh...  132 us

profile of v3, /device:TPU:1, one launch (start us, length us, event | category | flops | bytes accessed | tf_op | source)
XLA Modules:
  0.0 134.0 jit_solution(6426544009070285227)
XLA Ops:
  0.6 132.0 %shard_map.104 = (bf16[128,1792]{1,0:T(8,128)(2,1)S(1)}, f32[6,128]{1,0:T(8,128)S(1)}) custom-call(bf16[128,1792]{1,0:T(8,128)(2,1)} %x_ref.1, s32[4,128]{1,0:T(4,128)} %bitcast.7, s32[6,128]{1,0:T(8,128)} %bitcast.5, f32[6,128]{1,0:T(8,128)} %bitcast.6, bf16[2,1024,256]{2,1,0:T(8,128)(2,1)} %gate_pre_ref.1, bf16[2,1024,256]{2,1,0:T(8,128)(2,1)} %up_pre_ref.1, ...), custom_call_target="tpu_custom_call" | custom-call | tf_op jit(solution)/shard_map/pallas_call | solution.py:729
  132.6 0.8 copy.13
  133.4 0.6 copy.14

commit v4 on v3

--- a/solution.py
+++ b/solution.py
@@ -16,6 +16,8 @@
 EXTRA = 128
 EXPERTS = 32
 CHUNKS = (8, 8, 8, 8, 8, 8, 8, 8)
+DOWN_GROUPS = ((0,), (1,), (2,), (3, 4), (5, 6), (7,))
+UP_GROUPS = ((0, 1), (2, 3), (4, 5), (6,))
 
 
 def near(u):
@@ -64,10 +66,10 @@
 
 
 def kernel(
-    x_ref,
-    nodes_ref,
-    experts_ref,
-    probs_ref,
+    x_hbm,
+    nodes_hbm,
+    experts_hbm,
+    probs_hbm,
     gate_pre_ref,
     up_pre_ref,
     gate_w_ref,
@@ -80,6 +82,9 @@
     gate_w,
     up_w,
     down_w,
+    nodes_ref,
+    experts_ref,
+    probs_ref,
     table,
     column_node,
     column_slot,
@@ -131,7 +136,7 @@
     my, mx = n // SIDE, n % SIDE
     up = lax.rem(z + 1, SIDE)
     down = lax.rem(z + 3, SIDE)
-    tokens, width = x_ref.shape
+    tokens, width = x_hbm.shape
     rows_node = gate_pre.shape[1]
     hidden = gate_pre.shape[2]
     tiles = rows_node // TILE
@@ -173,10 +178,14 @@
                 (down_w_ref, down_w),
                 (gate_w_ref, gate_w),
                 (up_w_ref, up_w),
+                (nodes_hbm, nodes_ref),
+                (experts_hbm, experts_ref),
+                (probs_hbm, probs_ref),
+                (x_hbm, x_ext.at[:, pl.ds(0, width)]),
             )
         )
     ]
-    for load in loads:
+    for load in loads[5:]:
         load.start()
 
     barrier = pltpu.get_barrier_semaphore()
@@ -201,6 +210,11 @@
     @pl.loop(0, NODES)
     def _(o):
         greet(other, node_plus(o // SIDE, o % SIDE), z)
+
+    for load in loads[:5]:
+        load.start()
+    for load in loads[5:]:
+        load.wait()
 
     table[...] = jnp.zeros_like(table)
     table[0 : nodes_ref.shape[0], :] = nodes_ref[...].astype(jnp.float32)
@@ -214,7 +228,6 @@
             lane == table[:, 8 + k : 9 + k], table[:, 16 + k : 17 + k], 0.0
         )
     x_ext[:, width:] = mass.astype(jnp.bfloat16)
-    x_ext[:, :width] = x_ref[...]
     before = (
         lax.broadcasted_iota(jnp.int32, (tokens, tokens), 1)
         < lax.broadcasted_iota(jnp.int32, (tokens, tokens), 0)
@@ -246,14 +259,9 @@
         )
         chosen = jnp.where(position == column_slot[t : t + 1, :], member, 0.0)
         sel[t // 2, :, t % 2 * TILE : (t % 2 + 1) * TILE] = chosen.astype(jnp.bfloat16)
-        picked = chosen.T.astype(jnp.bfloat16)
-
-        @pl.loop(0, x_ext.shape[1] // 384)
-        def _(i):
-            features = pl.ds(pl.multiple_of(i * 384, 128), 384)
-            out_rows[t * TILE : (t + 1) * TILE, features] = jnp.dot(
-                picked, x_ext[:, features], preferred_element_type=jnp.float32
-            ).astype(jnp.bfloat16)
+        out_rows[t * TILE : (t + 1) * TILE, :] = jnp.dot(
+            chosen.T.astype(jnp.bfloat16), x_ext[...], preferred_element_type=jnp.float32
+        ).astype(jnp.bfloat16)
 
     pick(0)
     pl.semaphore_wait(barrier, 2 + (SIDE - 1) + (NODES - 1) + NODES)
@@ -350,12 +358,16 @@
     def gather_saved_on(_):
         gather_on(pre_full, 2, pl.ds(0, sizes[0]), pre_send, pre_recv, pre_far_recv)
 
-    def multiply_down(c):
-        begin, count = starts[c], sizes[c]
+    def chunk_rows(c):
+        return pl.ds(starts[c], sizes[c])
+
+    def multiply_down(g):
+        chunks = DOWN_GROUPS[g]
+        begin, count = starts[chunks[0]], sum(sizes[c] for c in chunks)
         rows = pl.ds(begin, count)
         for t in range(begin // TILE, (begin + count) // TILE):
             rows_arrived(t)
-        if c == 0:
+        if g == 0:
             loads[2].wait()
 
         def products(first, stop, step_of):
@@ -366,14 +378,27 @@
                 weights = down_w[e, quarter((z + step) % SIDE), :]
                 part[k, e, rows, :] = nt_dot(in_rows[rows, :width], weights).astype(jnp.bfloat16)
 
-        products(0, 1, lambda k: 2)
-        along_z(part.at[0, 0, rows], rs_far.at[0, rows], rs_send, rs_far_recv.at[c, 0], up)
-        along_z(part.at[0, 1, rows], rs_far.at[1, rows], rs_send, rs_far_recv.at[c, 1], down)
+        if g == 0:
+            one = chunk_rows(0)
+            for e, local in ((0, up), (1, down)):
+                weights = down_w[e, quarter((z + 2) % SIDE), :]
+                part[0, e, one, :] = nt_dot(in_rows[one, :width], weights).astype(jnp.bfloat16)
+                along_z(part.at[0, e, one], rs_far.at[e, one], rs_send, rs_far_recv.at[0, e], local)
+        else:
+            products(0, 1, lambda k: 2)
+        for c in chunks if g > 0 else ():
+            one = chunk_rows(c)
+            along_z(part.at[0, 0, one], rs_far.at[0, one], rs_send, rs_far_recv.at[c, 0], up)
+            along_z(part.at[0, 1, one], rs_far.at[1, one], rs_send, rs_far_recv.at[c, 1], down)
         products(1, 3, lambda k: 2 * k - 1)
-        along_z(part.at[1, 1, rows], rs_near.at[0, 1, rows], rs_send, rs_near_recv.at[c, 0, 1], up)
-        along_z(
-            part.at[2, 0, rows], rs_near.at[1, 0, rows], rs_send, rs_near_recv.at[c, 1, 0], down
-        )
+        for c in chunks:
+            one = chunk_rows(c)
+            along_z(
+                part.at[1, 1, one], rs_near.at[0, 1, one], rs_send, rs_near_recv.at[c, 0, 1], up
+            )
+            along_z(
+                part.at[2, 0, one], rs_near.at[1, 0, one], rs_send, rs_near_recv.at[c, 1, 0], down
+            )
         products(3, 4, lambda k: 0)
 
     def add_far(c):
@@ -526,8 +551,9 @@
 
     cut = width // 256 // 2 + 1
 
-    def multiply_up(c, first, stop):
-        rows = pl.ds(starts[c], sizes[c])
+    def multiply_up(g, first, stop):
+        chunks = UP_GROUPS[g]
+        rows = pl.ds(starts[chunks[0]], sum(sizes[c] for c in chunks))
 
         @pl.loop(first, stop)
         def _(i):
@@ -536,14 +562,16 @@
                 jnp.bfloat16
             )
 
-        send_back(c, pl.ds(first * 256, (stop - first) * 256))
-
-    def multiply_up_low(c):
-        await_grads(c)
-        multiply_up(c, 0, cut)
-
-    def multiply_up_high(c):
-        multiply_up(c, cut, width // 256)
+        for c in chunks:
+            send_back(c, pl.ds(first * 256, (stop - first) * 256))
+
+    def multiply_up_low(g):
+        for c in UP_GROUPS[g]:
+            await_grads(c)
+        multiply_up(g, 0, cut)
+
+    def multiply_up_high(g):
+        multiply_up(g, cut, width // 256)
 
     def multiply_up_own(c):
         rows = pl.ds(starts[c], sizes[c])
@@ -628,61 +656,53 @@
         (send_rows, 2),
         (send_rows, 3),
         (send_rows, 4),
+        (gather_saved_on, 0),
         (multiply_down, 0),
-        (gather_saved_on, 0),
+        (multiply_down, 1),
         (add_far, 0),
-        (multiply_down, 1),
+        (add_far, 1),
+        (multiply_down, 2),
+        (hidden_grads, 0),
         (send_rows, 5),
-        (hidden_grads, 0),
-        (multiply_down, 2),
-        (add_far, 1),
+        (add_far, 2),
+        (send_rows, 6),
+        (hidden_grads, 1),
+        (hidden_grads, 2),
+        (multiply_down, 3),
+        (send_on, 1),
         (send_on, 0),
-        (multiply_down, 3),
-        (hidden_grads, 1),
-        (add_far, 2),
+        (send_rows, 7),
+        (add_far, 3),
+        (add_far, 4),
+        (multiply_down, 4),
+        (hidden_grads, 3),
         (multiply_up_low, 0),
-        (add_far, 3),
-        (send_on, 1),
-        (multiply_down, 4),
-        (hidden_grads, 2),
-        (multiply_down, 5),
-        (send_rows, 6),
+        (add_far, 5),
+        (send_on, 3),
+        (send_on, 2),
+        (hidden_grads, 5),
+        (hidden_grads, 4),
         (multiply_up_high, 0),
-        (add_far, 4),
-        (send_on, 2),
-        (hidden_grads, 3),
-        (send_rows, 7),
+        (add_far, 6),
         (multiply_up_low, 1),
         (multiply_up_high, 1),
-        (hidden_grads, 4),
-        (add_far, 5),
+        (send_on, 5),
+        (send_on, 4),
+        (combine, 0),
+        (multiply_down, 5),
+        (hidden_grads, 6),
         (multiply_up_low, 2),
-        (send_on, 3),
-        (multiply_down, 6),
-        (multiply_down, 7),
+        (add_far, 7),
+        (send_on, 6),
         (multiply_up_high, 2),
-        (send_on, 4),
-        (hidden_grads, 5),
-        (multiply_up_low, 3),
-        (multiply_up_high, 3),
-        (add_far, 6),
-        (multiply_up_low, 4),
-        (send_on, 5),
-        (add_far, 7),
-        (multiply_up_high, 4),
-        (hidden_grads, 6),
-        (combine, 0),
-        (multiply_up_low, 5),
-        (send_on, 6),
         (hidden_grads, 7),
         (multiply_up_own, 7),
-        (multiply_up_high, 5),
-        (multiply_up_low, 6),
+        (multiply_up_low, 3),
         (send_on, 7),
-        (multiply_up_high, 6),
+        (multiply_up_high, 3),
         (multiply_up_near, 7),
+        (multiply_up_far, 7),
         (sum_prob, 0),
-        (multiply_up_far, 7),
         (combine, 1),
         (combine, 2),
     ):
@@ -729,7 +749,7 @@
     handed, prob = pl.pallas_call(
         kernel,
         out_shape=results,
-        in_specs=[in_vmem] * 4 + [anywhere] * 5,
+        in_specs=[anywhere] * 9,
         out_specs=(in_vmem, in_vmem),
         scratch_shapes=[
             pltpu.VMEM(gate_pre.shape, half),
@@ -737,6 +757,9 @@
             pltpu.VMEM(gate_w.shape, half),
             pltpu.VMEM(up_w.shape, half),
             pltpu.VMEM(down_w.shape, half),
+            pltpu.VMEM(node_ids.shape[::-1], jnp.int32),
+            pltpu.VMEM(expert_ids.shape[::-1], jnp.int32),
+            pltpu.VMEM(gate_probs.shape[::-1], single),
             pltpu.VMEM((tokens, tokens), single),
             pltpu.VMEM((rows // TILE, TILE), single),
             pltpu.VMEM((rows // TILE, TILE), single),
@@ -759,7 +782,7 @@
             pltpu.VMEM((tokens, width), single),
             pltpu.VMEM((tokens, EXTRA), single),
             pltpu.VMEM((SIDE, tokens, EXTRA), single),
-            dma((5,)),
+            dma((9,)),
             dma,
             dma((rows // TILE,)),
             dma,

time: 134 us -> 134 us (level)
  no operation moved by 1% of the time
where the time goes in v4:
time: 134 us
  Pallas kernels  132 us (99%)
  local copies, waits for them, and re-layouts  1.36 us (1%)
    pallas_call x1, Pallas kernels, shards(): pl.pallas_call(kernel, out_shape=results, in_specs=[anywhere] * 9, out_sp...  132 us

profile of v4, /device:TPU:1, one launch (start us, length us, event | category | flops | bytes accessed | tf_op | source)
XLA Modules:
  0.0 134.3 jit_solution(1759421442295086331)
XLA Ops:
  0.6 132.3 %shard_map.104 = (bf16[128,1792]{1,0:T(8,128)(2,1)S(1)}, f32[6,128]{1,0:T(8,128)S(1)}) custom-call(bf16[128,1792]{1,0:T(8,128)(2,1)} %x_hbm.1, s32[4,128]{1,0:T(4,128)} %bitcast.7, s32[6,128]{1,0:T(8,128)} %bitcast.5, f32[6,128]{1,0:T(8,128)} %bitcast.6, bf16[2,1024,256]{2,1,0:T(8,128)(2,1)} %gate_pre_ref.1, bf16[2,1024,256]{2,1,0:T(8,128)(2,1)} %up_pre_ref.1, ...), custom_call_target="tpu_custom_call" | custom-call | tf_op jit(solution)/shard_map/pallas_call | solution.py:749
  132.9 0.8 copy.13
  133.7 0.6 copy.14
